TPU v7x, 32 devices: a whole 2x2x4 slice. The times are simulated.
32 devices in a mesh: node: 4 (over x, core), chip: 8 (over z, y).
Axes of the slice: x: 2, y: 2, z: 4, core: 2. Of those that a mesh axis runs over, the one named last changes fastest.
Arguments:
- tokens: bfloat16 [128, 145, 1024], P(('node', 'chip')), may hold values from -6 to 6
- cotangent: bfloat16 [128, 145, 1024], P(('node', 'chip')), may hold values from -6 to 6
- w_attn_in: float32 [2, 1024, 3072], P(None, ('node', 'chip')), may hold values from -0.1875 to 0.1875
- w_attn_out: float32 [2, 1024, 1024], P(None, ('node', 'chip')), may hold values from -0.5 to 0.5
- w_mlp_in: float32 [2, 1024, 4096], P(None, ('node', 'chip')), may hold values from -0.1875 to 0.1875
- w_mlp_out: float32 [2, 4096, 1024], P(None, ('node', 'chip')), may hold values from -0.09375 to 0.09375
- vectors: float32 [2, 14336], P(None, ('node', 'chip')), may hold values from -1.5 to 1.5
- first_attn_in: float32 [2, 1024, 3072], P(None, ('node', 'chip')), may hold values from -28 to 28
- first_attn_out: float32 [2, 1024, 1024], P(None, ('node', 'chip')), may hold values from -28 to 28
- first_mlp_in: float32 [2, 1024, 4096], P(None, ('node', 'chip')), may hold values from -32 to 32
- first_mlp_out: float32 [2, 4096, 1024], P(None, ('node', 'chip')), may hold values from -64 to 64
- first_vectors: float32 [2, 14336], P(None, ('node', 'chip')), may hold values from -96 to 96
- second_attn_in: float32 [2, 1024, 3072], P(None, ('node', 'chip')), may hold values from 0.8352 to 13.3632
- second_attn_out: float32 [2, 1024, 1024], P(None, ('node', 'chip')), may hold values from 0.8352 to 13.3632
- second_mlp_in: float32 [2, 1024, 4096], P(None, ('node', 'chip')), may hold values from 1.1368 to 18.1888
- second_mlp_out: float32 [2, 4096, 1024], P(None, ('node', 'chip')), may hold values from 4.5472 to 72.7552
- second_vectors: float32 [2, 14336], P(None, ('node', 'chip')), may hold values from 9.28 to 148.48
Outputs:
- output: bfloat16 [128, 145, 1024], P(('node', 'chip'))
- d_tokens: float32 [128, 145, 1024], P(('node', 'chip'))
- new_attn_in: float32 [2, 1024, 3072], P(None, ('node', 'chip'))
- new_attn_out: float32 [2, 1024, 1024], P(None, ('node', 'chip'))
- new_mlp_in: float32 [2, 1024, 4096], P(None, ('node', 'chip'))
- new_mlp_out: float32 [2, 4096, 1024], P(None, ('node', 'chip'))
- new_vectors: float32 [2, 14336], P(None, ('node', 'chip'))
- new_first_attn_in: float32 [2, 1024, 3072], P(None, ('node', 'chip'))
- new_first_attn_out: float32 [2, 1024, 1024], P(None, ('node', 'chip'))
- new_first_mlp_in: float32 [2, 1024, 4096], P(None, ('node', 'chip'))
- new_first_mlp_out: float32 [2, 4096, 1024], P(None, ('node', 'chip'))
- new_first_vectors: float32 [2, 14336], P(None, ('node', 'chip'))
- new_second_attn_in: float32 [2, 1024, 3072], P(None, ('node', 'chip'))
- new_second_attn_out: float32 [2, 1024, 1024], P(None, ('node', 'chip'))
- new_second_mlp_in: float32 [2, 1024, 4096], P(None, ('node', 'chip'))
- new_second_mlp_out: float32 [2, 4096, 1024], P(None, ('node', 'chip'))
- new_second_vectors: float32 [2, 14336], P(None, ('node', 'chip'))
All inputs are finite; a program needn't handle non-finite values.
Results may differ from a plain program's by a relative error of at most 0.012.
The roundings to bfloat16 on the way count: a program that leaves them out, or rounds other values in their place, can miss the bound.
Values may be sent and summed in bfloat16 or wider, within the bound.
A program may use at most 320 MiB of HBM per device.

v0:
```python
import math

import jax
import jax.numpy as jnp
from jax import lax
from jax.sharding import PartitionSpec as P

D = 1024
HEADS = 16
HEAD_DIM = 64
FF = 4096
STEP = 10
SEQ = 145


norm_eps = 1e-06
beta_first = 0.9
beta_second = 0.999
adam_eps = 1e-08


def norm_forward(values, gain_row, shift_row):
    centre = jnp.mean(values, axis=-1, keepdims=True)
    centred = values - centre
    spread = jnp.mean(centred * centred, axis=-1, keepdims=True)
    inverse = lax.rsqrt(spread + norm_eps)
    normal = centred * inverse
    return (normal * gain_row + shift_row, normal, inverse)


def norm_backward(upstream, normal, inverse, gain_row):
    d_gain = jnp.sum(upstream * normal, axis=0)
    d_shift = jnp.sum(upstream, axis=0)
    scaled = upstream * gain_row
    inner = (
        scaled
        - jnp.mean(scaled, axis=-1, keepdims=True)
        - normal * jnp.mean(scaled * normal, axis=-1, keepdims=True)
    )
    return (inverse * inner, d_gain, d_shift)


def split_vector(vector_row):
    pieces = [vector_row[index * D : (index + 1) * D] for index in range(10)]
    return pieces + [vector_row[10 * D :]]


def attend_scores(query_b, key_b):
    return jnp.einsum(
        "gqhc,gkhc->ghqk", query_b, key_b, preferred_element_type=jnp.float32
    ) * HEAD_DIM ** (-0.5)


def forward_layer(hidden, matrices, vector_row):
    w_in, w_out, w_up, w_down = matrices
    gain_a, shift_a, bias_q, bias_v, bias_o, scale_a, gain_m, shift_m, bias_d, scale_m, bias_u = (
        split_vector(vector_row)
    )
    images = hidden.shape[0] // SEQ
    heads_shape = (images, SEQ, HEADS, HEAD_DIM)
    normed_a, normal_a, inverse_a = norm_forward(hidden, gain_a, shift_a)
    normed_a_b = normed_a.astype(jnp.bfloat16)
    projected = jnp.dot(normed_a_b, w_in, preferred_element_type=jnp.float32)
    projected = projected + jnp.concatenate([bias_q, jnp.zeros_like(bias_q), bias_v])
    query_b = projected[:, :D].astype(jnp.bfloat16).reshape(heads_shape)
    key_b = projected[:, D : 2 * D].astype(jnp.bfloat16).reshape(heads_shape)
    value_b = projected[:, 2 * D :].astype(jnp.bfloat16).reshape(heads_shape)
    scores = attend_scores(query_b, key_b)
    top_score = jnp.max(scores, axis=-1, keepdims=True)
    expo = jnp.exp(scores - top_score)
    total = jnp.sum(expo, axis=-1, keepdims=True)
    probs_b = (expo / total).astype(jnp.bfloat16)
    log_total = top_score + jnp.log(total)
    mixed = jnp.einsum("ghqk,gkhc->gqhc", probs_b, value_b, preferred_element_type=jnp.float32)
    mixed_b = mixed.reshape(-1, D).astype(jnp.bfloat16)
    branch = jnp.dot(mixed_b, w_out, preferred_element_type=jnp.float32) + bias_o
    middle = hidden + scale_a * branch
    normed_m, normal_m, inverse_m = norm_forward(middle, gain_m, shift_m)
    normed_m_b = normed_m.astype(jnp.bfloat16)
    upper = jnp.dot(normed_m_b, w_up, preferred_element_type=jnp.float32) + bias_u
    active_b = jax.nn.gelu(upper, approximate=False).astype(jnp.bfloat16)
    down = jnp.dot(active_b, w_down, preferred_element_type=jnp.float32) + bias_d
    result = middle + scale_m * down
    saved = (
        normal_a,
        inverse_a,
        normed_a_b,
        query_b,
        key_b,
        value_b,
        log_total,
        mixed_b,
        branch,
        normal_m,
        inverse_m,
        normed_m_b,
        upper,
        active_b,
        down,
    )
    return (result, saved)


def backward_layer(upstream, saved, matrices, vector_row):
    w_in, w_out, w_up, w_down = matrices
    gain_a, shift_a, bias_q, bias_v, bias_o, scale_a, gain_m, shift_m, bias_d, scale_m, bias_u = (
        split_vector(vector_row)
    )
    (
        normal_a,
        inverse_a,
        normed_a_b,
        query_b,
        key_b,
        value_b,
        log_total,
        mixed_b,
        branch,
        normal_m,
        inverse_m,
        normed_m_b,
        upper,
        active_b,
        down,
    ) = saved
    d_scale_m = jnp.sum(upstream * down, axis=0)
    d_down = upstream * scale_m
    d_bias_d = jnp.sum(d_down, axis=0)
    d_down_b = d_down.astype(jnp.bfloat16)
    g_down = jnp.einsum("tf,td->fd", active_b, d_down_b, preferred_element_type=jnp.float32)
    d_active = jnp.einsum("td,fd->tf", d_down_b, w_down, preferred_element_type=jnp.float32)
    cumulative = 0.5 * (1.0 + lax.erf(upper * 0.5**0.5))
    density = jnp.exp(-0.5 * upper * upper) * (2.0 * math.pi) ** (-0.5)
    d_upper = d_active * (cumulative + upper * density)
    d_bias_u = jnp.sum(d_upper, axis=0)
    d_upper_b = d_upper.astype(jnp.bfloat16)
    g_up = jnp.einsum("td,tf->df", normed_m_b, d_upper_b, preferred_element_type=jnp.float32)
    d_normed_m = jnp.einsum("tf,df->td", d_upper_b, w_up, preferred_element_type=jnp.float32)
    d_middle, d_gain_m, d_shift_m = norm_backward(d_normed_m, normal_m, inverse_m, gain_m)
    d_middle = d_middle + upstream
    d_scale_a = jnp.sum(d_middle * branch, axis=0)
    d_branch = d_middle * scale_a
    d_bias_o = jnp.sum(d_branch, axis=0)
    d_branch_b = d_branch.astype(jnp.bfloat16)
    g_out = jnp.einsum("td,te->de", mixed_b, d_branch_b, preferred_element_type=jnp.float32)
    d_mixed_b = jnp.einsum(
        "te,de->td", d_branch_b, w_out, preferred_element_type=jnp.float32
    ).astype(jnp.bfloat16)
    d_mixed_b = d_mixed_b.reshape(query_b.shape)
    scores = attend_scores(query_b, key_b)
    probs = jnp.exp(scores - log_total)
    probs_b = probs.astype(jnp.bfloat16)
    d_probs = jnp.einsum("gqhc,gkhc->ghqk", d_mixed_b, value_b, preferred_element_type=jnp.float32)
    d_value = jnp.einsum("ghqk,gqhc->gkhc", probs_b, d_mixed_b, preferred_element_type=jnp.float32)
    d_scores = probs * (d_probs - jnp.sum(probs * d_probs, axis=-1, keepdims=True))
    d_scores_b = d_scores.astype(jnp.bfloat16)
    d_query = jnp.einsum(
        "ghqk,gkhc->gqhc", d_scores_b, key_b, preferred_element_type=jnp.float32
    ) * HEAD_DIM ** (-0.5)
    d_key = jnp.einsum(
        "ghqk,gqhc->gkhc", d_scores_b, query_b, preferred_element_type=jnp.float32
    ) * HEAD_DIM ** (-0.5)
    rows = upstream.shape[0]
    d_query = d_query.reshape(rows, D)
    d_value = d_value.reshape(rows, D)
    d_projected = jnp.concatenate([d_query, d_key.reshape(rows, D), d_value], axis=1)
    d_bias_q = jnp.sum(d_query, axis=0)
    d_bias_v = jnp.sum(d_value, axis=0)
    d_projected_b = d_projected.astype(jnp.bfloat16)
    g_in = jnp.einsum("td,te->de", normed_a_b, d_projected_b, preferred_element_type=jnp.float32)
    d_normed_a = jnp.einsum("te,de->td", d_projected_b, w_in, preferred_element_type=jnp.float32)
    d_hidden, d_gain_a, d_shift_a = norm_backward(d_normed_a, normal_a, inverse_a, gain_a)
    d_hidden = d_hidden + d_middle
    d_vector = jnp.concatenate(
        [
            d_gain_a,
            d_shift_a,
            d_bias_q,
            d_bias_v,
            d_bias_o,
            d_scale_a,
            d_gain_m,
            d_shift_m,
            d_bias_d,
            d_scale_m,
            d_bias_u,
        ]
    )
    return (d_hidden, (g_in, g_out, g_up, g_down, d_vector))


def fetch_forward(shards, layer_index):
    attn_in, attn_out, mlp_in, mlp_out, vector_row = [
        member[layer_index].astype(jnp.bfloat16) for member in shards
    ]
    return (
        lax.all_gather(attn_in, ("node", "chip"), axis=0, tiled=True),
        lax.all_gather(attn_out, ("node", "chip"), axis=0, tiled=True),
        lax.all_gather(mlp_in, ("node", "chip"), axis=0, tiled=True),
        lax.all_gather(mlp_out, ("node", "chip"), axis=0, tiled=True),
        lax.all_gather(vector_row, ("node", "chip"), axis=0, tiled=True),
    )


def fetch_backward(shards, layer_index):
    attn_in, attn_out, mlp_in, mlp_out, vector_row = [
        member[layer_index].astype(jnp.bfloat16) for member in shards
    ]
    return (
        lax.all_gather(attn_in, ("node", "chip"), axis=0, tiled=True),
        lax.all_gather(attn_out, ("node", "chip"), axis=0, tiled=True),
        lax.all_gather(mlp_in, ("node", "chip"), axis=0, tiled=True),
        lax.all_gather(mlp_out, ("node", "chip"), axis=0, tiled=True),
        lax.all_gather(vector_row, ("node", "chip"), axis=0, tiled=True),
    )


def adamw(weight, gradient, first, second, rate, decay):
    first_new = beta_first * first + (1.0 - beta_first) * gradient
    second_new = beta_second * second + (1.0 - beta_second) * gradient * gradient
    fix_first = 1.0 - beta_first**STEP
    fix_second = 1.0 - beta_second**STEP
    stepped = first_new / fix_first / (jnp.sqrt(second_new / fix_second) + adam_eps)
    return (weight - rate * (stepped + decay * weight), first_new, second_new)


def on_device(
    tokens,
    cotangent,
    w_attn_in,
    w_attn_out,
    w_mlp_in,
    w_mlp_out,
    vectors,
    first_attn_in,
    first_attn_out,
    first_mlp_in,
    first_mlp_out,
    first_vectors,
    second_attn_in,
    second_attn_out,
    second_mlp_in,
    second_mlp_out,
    second_vectors,
):
    shards = (w_attn_in, w_attn_out, w_mlp_in, w_mlp_out, vectors)
    layers = w_attn_in.shape[0]
    token_rows = tokens.shape[0] * tokens.shape[1]
    hidden = tokens.astype(jnp.float32).reshape(token_rows, D)
    kept_values = []
    for layer_index in range(layers):
        gathered = fetch_forward(shards, layer_index)
        hidden, saved = forward_layer(hidden, gathered[:4], gathered[4].astype(jnp.float32))
        kept_values.append(saved)
    output = hidden.reshape(tokens.shape).astype(jnp.bfloat16)
    upstream = cotangent.astype(jnp.float32).reshape(token_rows, D)
    collected = [None] * layers
    for layer_index in reversed(range(layers)):
        gathered = fetch_backward(shards, layer_index)
        upstream, terms = backward_layer(
            upstream, kept_values[layer_index], gathered[:4], gathered[4].astype(jnp.float32)
        )
        collected[layer_index] = (
            lax.psum_scatter(terms[0], ("node", "chip"), scatter_dimension=0, tiled=True),
            lax.psum_scatter(terms[1], ("node", "chip"), scatter_dimension=0, tiled=True),
            lax.psum_scatter(terms[2], ("node", "chip"), scatter_dimension=0, tiled=True),
            lax.psum_scatter(terms[3], ("node", "chip"), scatter_dimension=0, tiled=True),
            lax.psum_scatter(terms[4], ("node", "chip"), scatter_dimension=0, tiled=True),
        )
    stacked = [
        jnp.stack([collected[layer_index][member] for layer_index in range(layers)])
        for member in range(5)
    ]
    firsts = (first_attn_in, first_attn_out, first_mlp_in, first_mlp_out, first_vectors)
    seconds = (second_attn_in, second_attn_out, second_mlp_in, second_mlp_out, second_vectors)
    settings = (
        (D ** (-0.5), 0.05),
        ((D // 8) ** (-0.5), 0.05),
        (D ** (-0.5), 0.05),
        (FF ** (-0.5), 0.05),
        (0.3, 0.0),
    )
    updated = [
        adamw(
            shards[member],
            stacked[member],
            firsts[member],
            seconds[member],
            settings[member][0],
            settings[member][1],
        )
        for member in range(5)
    ]
    d_tokens = upstream.reshape(tokens.shape)
    return (
        output,
        d_tokens,
        updated[0][0],
        updated[1][0],
        updated[2][0],
        updated[3][0],
        updated[4][0],
        updated[0][1],
        updated[1][1],
        updated[2][1],
        updated[3][1],
        updated[4][1],
        updated[0][2],
        updated[1][2],
        updated[2][2],
        updated[3][2],
        updated[4][2],
    )


def solution(mesh):
    in_specs = (
        P(("node", "chip"), None, None),
        P(("node", "chip"), None, None),
        P(None, ("node", "chip"), None),
        P(None, ("node", "chip"), None),
        P(None, ("node", "chip"), None),
        P(None, ("node", "chip"), None),
        P(None, ("node", "chip")),
        P(None, ("node", "chip"), None),
        P(None, ("node", "chip"), None),
        P(None, ("node", "chip"), None),
        P(None, ("node", "chip"), None),
        P(None, ("node", "chip")),
        P(None, ("node", "chip"), None),
        P(None, ("node", "chip"), None),
        P(None, ("node", "chip"), None),
        P(None, ("node", "chip"), None),
        P(None, ("node", "chip")),
    )
    out_specs = (
        P(("node", "chip"), None, None),
        P(("node", "chip"), None, None),
        P(None, ("node", "chip"), None),
        P(None, ("node", "chip"), None),
        P(None, ("node", "chip"), None),
        P(None, ("node", "chip"), None),
        P(None, ("node", "chip")),
        P(None, ("node", "chip"), None),
        P(None, ("node", "chip"), None),
        P(None, ("node", "chip"), None),
        P(None, ("node", "chip"), None),
        P(None, ("node", "chip")),
        P(None, ("node", "chip"), None),
        P(None, ("node", "chip"), None),
        P(None, ("node", "chip"), None),
        P(None, ("node", "chip"), None),
        P(None, ("node", "chip")),
    )
    return jax.shard_map(
        on_device, mesh=mesh, in_specs=in_specs, out_specs=out_specs, check_vma=False
    )
```

profile of v0, /device:TPU:0, one launch (start us, length us, event | category | flops | bytes accessed | tf_op | source)
XLA Modules:
  0.0 3000.6 jit_solution(2174315051506841222)
XLA Ops:
  16.4 43.0 %all-reduce.5 = (bf16[14336]{0:T(1024)(128)(2,1)S(1)}, bf16[14336]{0:T(1024)(128)(2,1)S(1)}) all-reduce(bf16[14336]{0:T(1024)(128)(2,1)S(1)} %dynamic-update-slice, bf16[14336]{0:T(1024)(128)(2,1)S(1)} %dynamic-update-slice.1), channel_id=2, replica_groups=mesh['node'=4,'chip'=8] {'node','chip'}, use_global_device_ids=true, to_apply=%add | all-reduce | flops 28672 | bytes 114688
  148.7 73.6 %all-gather.23.cloned.1.call-done = bf16[1,1024,4096]{2,1,0:T(8,128)(2,1)} async-done(((bf16[1,32,4096]{2,1,0:T(8,128)(2,1)}), bf16[1,1024,4096]{2,1,0:T(8,128)(2,1)}) %all-gather.23.cloned.1.call-update) | async-done | bytes 8388624 | tf_op jit(solution)/shard_map/all_gather | solution.py:199
  222.4 30.7 %fusion.2 = (bf16[580,4096]{1,0:T(8,128)(2,1)}, f32[580,4096]{1,0:T(8,128)}) fusion(f32[4096]{0:T(1024)S(1)} %bitcast.234, bf16[1,1024,4096]{2,1,0:T(8,128)(2,1)} %all-gather.23.cloned.1.call-done, f32[580,1024]{1,0:T(8,128)S(1)} %get-tuple-element.136, f32[1024]{0:T(1024)S(1)} %bitcast.196, f32[1024]{0:T(1024)S(1)} %bitcast.190, ...), kind=kOutput, calls=%fused_computation.16 | convolution fusion | flops 5025157120 | bytes 25047584 | tf_op jit(solution)/shard_map/dot_general | solution.py:80
  253.1 48.6 %all-gather.25.cloned.1.call-done = bf16[1,4096,1024]{2,1,0:T(8,128)(2,1)} async-done(((bf16[1,128,1024]{2,1,0:T(8,128)(2,1)}), bf16[1,4096,1024]{2,1,0:T(8,128)(2,1)}) %all-gather.25.cloned.1.call-update) | async-done | bytes 8388624 | tf_op jit(solution)/shard_map/all_gather | solution.py:200
  313.6 59.5 %all-gather.27.cloned.1.call-done = bf16[1,1024,3072]{2,1,0:T(8,128)(2,1)} async-done(((bf16[1,32,3072]{2,1,0:T(8,128)(2,1)}), bf16[1,1024,3072]{2,1,0:T(8,128)(2,1)}) %all-gather.27.cloned.1.call-update) | async-done | bytes 6291472 | tf_op jit(solution)/shard_map/all_gather | solution.py:197
  437.7 73.7 %all-gather.31.cloned.1.call-done = bf16[1,1024,4096]{2,1,0:T(8,128)(2,1)} async-done(((bf16[1,32,4096]{2,1,0:T(8,128)(2,1)}), bf16[1,1024,4096]{2,1,0:T(8,128)(2,1)}) %all-gather.31.cloned.1.call-update) | async-done | bytes 8388624 | tf_op jit(solution)/shard_map/all_gather | solution.py:199
  511.4 31.0 %fusion.5 = (bf16[580,4096]{1,0:T(8,128)(2,1)}, f32[580,4096]{1,0:T(8,128)}) fusion(f32[4096]{0:T(1024)S(1)} %bitcast.236, bf16[1,1024,4096]{2,1,0:T(8,128)(2,1)} %all-gather.31.cloned.1.call-done, f32[580,1024]{1,0:T(8,128)S(1)} %get-tuple-element.132, f32[1024]{0:T(1024)S(1)} %bitcast.198, f32[1024]{0:T(1024)S(1)} %bitcast.200, ...), kind=kOutput, calls=%fused_computation.19 | convolution fusion | flops 5025157120 | bytes 25047584 | tf_op jit(solution)/shard_map/dot_general | solution.py:80
  542.4 48.6 %all-gather.33.cloned.1.call-done = bf16[1,4096,1024]{2,1,0:T(8,128)(2,1)} async-done(((bf16[1,128,1024]{2,1,0:T(8,128)(2,1)}), bf16[1,4096,1024]{2,1,0:T(8,128)(2,1)}) %all-gather.33.cloned.1.call-update) | async-done | bytes 8388624 | tf_op jit(solution)/shard_map/all_gather | solution.py:200
  591.0 13.2 fusion.131
  651.5 11.7 multiply_convert_fusion.1
  705.7 12.9 fusion.132
  756.2 11.7 multiply_convert_fusion
  859.0 13.0 fusion.76
  873.7 13.2 fusion.79
  888.6 12.7 fusion.102
  903.0 12.9 fusion.104
  943.9 145.4 %reduce-scatter.15.cloned.1.call-done = f32[32,1024]{1,0:T(8,128)} async-done(((f32[1024,1024]{1,0:T(8,128)}), f32[32,1024]{1,0:T(8,128)}) %reduce-scatter.15.cloned.1.call-update) | async-done | bytes 131088 | tf_op jit(solution)/shard_map/reduce_scatter | solution.py:265
  1089.3 142.8 %reduce-scatter.13.cloned.1.call-done = f32[32,1024]{1,0:T(8,128)} async-done(((f32[1024,1024]{1,0:T(8,128)}), f32[32,1024]{1,0:T(8,128)}) %reduce-scatter.13.cloned.1.call-update) | async-done | bytes 131088 | tf_op jit(solution)/shard_map/reduce_scatter | solution.py:265
  1234.4 156.2 %reduce-scatter.11.cloned.1.call-done = f32[32,3072]{1,0:T(8,128)} async-done(((f32[1024,3072]{1,0:T(8,128)}), f32[32,3072]{1,0:T(8,128)}) %reduce-scatter.11.cloned.1.call-update) | async-done | bytes 393232 | tf_op jit(solution)/shard_map/reduce_scatter | solution.py:264
  1390.6 161.5 %reduce-scatter.9.cloned.1.call-done = f32[32,3072]{1,0:T(8,128)} async-done(((f32[1024,3072]{1,0:T(8,128)}), f32[32,3072]{1,0:T(8,128)}) %reduce-scatter.9.cloned.1.call-update) | async-done | bytes 393232 | tf_op jit(solution)/shard_map/reduce_scatter | solution.py:264
  1555.5 356.0 %reduce-scatter.17.cloned.1.call-done = f32[32,4096]{1,0:T(8,128)} async-done(((f32[1024,4096]{1,0:T(8,128)}), f32[32,4096]{1,0:T(8,128)}) %reduce-scatter.17.cloned.1.call-update) | async-done | bytes 524304 | tf_op jit(solution)/shard_map/reduce_scatter | solution.py:266
  1911.5 359.5 %reduce-scatter.19.cloned.1.call-done = f32[32,4096]{1,0:T(8,128)} async-done(((f32[1024,4096]{1,0:T(8,128)}), f32[32,4096]{1,0:T(8,128)}) %reduce-scatter.19.cloned.1.call-update) | async-done | bytes 524304 | tf_op jit(solution)/shard_map/reduce_scatter | solution.py:266
  2275.1 355.3 %reduce-scatter.21.cloned.1.call-done = f32[128,1024]{1,0:T(8,128)} async-done(((f32[4096,1024]{1,0:T(8,128)}), f32[128,1024]{1,0:T(8,128)}) %reduce-scatter.21.cloned.1.call-update) | async-done | bytes 524304 | tf_op jit(solution)/shard_map/reduce_scatter | solution.py:267
  2630.5 359.5 %reduce-scatter.23.cloned.1.call-done = f32[128,1024]{1,0:T(8,128)} async-done(((f32[4096,1024]{1,0:T(8,128)}), f32[128,1024]{1,0:T(8,128)}) %reduce-scatter.23.cloned.1.call-update) | async-done | bytes 524304 | tf_op jit(solution)/shard_map/reduce_scatter | solution.py:267
  (455 shorter events, 438.6 us)
Async XLA Ops:
  7.2 76.8 %all-gather.19.cloned.1.call-start = ((), (), s32[]{:S(2)}) async-start(), calls=%async_computation.16 | async-start | bytes 6488064 | tf_op jit(solution)/shard_map/all_gather | solution.py:197
  9.4 133.2 %all-gather.21.cloned.1.call-start = ((), (), s32[]{:S(2)}) async-start(), calls=%async_computation.17 | async-start | bytes 2162688 | tf_op jit(solution)/shard_map/all_gather | solution.py:198
  11.1 211.3 %all-gather.23.cloned.1.call-start = ((), (), s32[]{:S(2)}) async-start(), calls=%async_computation.18 | async-start | bytes 8650752 | tf_op jit(solution)/shard_map/all_gather | solution.py:199
  12.1 289.6 %all-gather.25.cloned.1.call-start = ((), (), s32[]{:S(2)}) async-start(), calls=%async_computation.19 | async-start | bytes 8650752 | tf_op jit(solution)/shard_map/all_gather | solution.py:200
  13.1 360.1 %all-gather.27.cloned.1.call-start = ((), (), s32[]{:S(2)}) async-start(), calls=%async_computation.20 | async-start | bytes 6488064 | tf_op jit(solution)/shard_map/all_gather | solution.py:197
  13.6 417.9 %all-gather.29.cloned.1.call-start = ((), (), s32[]{:S(2)}) async-start(), calls=%async_computation.21 | async-start | bytes 2162688 | tf_op jit(solution)/shard_map/all_gather | solution.py:198
  14.2 497.2 %all-gather.31.cloned.1.call-start = ((), (), s32[]{:S(2)}) async-start(), calls=%async_computation.22 | async-start | bytes 8650752 | tf_op jit(solution)/shard_map/all_gather | solution.py:199
  15.0 576.0 %all-gather.33.cloned.1.call-start = ((), (), s32[]{:S(2)}) async-start(), calls=%async_computation.23 | async-start | bytes 8650752 | tf_op jit(solution)/shard_map/all_gather | solution.py:200
  15.7 926.0 %all-reduce.8.cloned.1.call-start = ((), (), s32[]{:S(2)}) async-start(), calls=%async_computation.24 | async-start | bytes 229376
  60.7 312.4 %copy-start.85 = (f32[1,1024]{1,0:T(1,128)}, f32[1,1024]{1,0:T(1,128)S(1)}, u32[]{:S(2)}) copy-start(f32[1,1024]{1,0:T(1,128)S(1)} %get-tuple-element.163) | copy-start | bytes 12292
  60.7 312.4 %copy-start.108 = (f32[1,1024]{1,0:T(1,128)}, f32[1,1024]{1,0:T(1,128)S(1)}, u32[]{:S(2)}) copy-start(f32[1,1024]{1,0:T(1,128)S(1)} %get-tuple-element.162) | copy-start | bytes 12292
  821.8 267.5 %reduce-scatter.15.cloned.1.call-start = ((), (), s32[]{:S(2)}) async-start(), calls=%async_computation.11 | async-start | bytes 4325376 | tf_op jit(solution)/shard_map/reduce_scatter | solution.py:265
  827.7 404.5 %reduce-scatter.13.cloned.1.call-start = ((), (), s32[]{:S(2)}) async-start(), calls=%async_computation.10 | async-start | bytes 4325376 | tf_op jit(solution)/shard_map/reduce_scatter | solution.py:265
  833.7 556.9 %reduce-scatter.11.cloned.1.call-start = ((), (), s32[]{:S(2)}) async-start(), calls=%async_computation.9 | async-start | bytes 12976128 | tf_op jit(solution)/shard_map/reduce_scatter | solution.py:264
  846.1 706.1 %reduce-scatter.9.cloned.1.call-start = ((), (), s32[]{:S(2)}) async-start(), calls=%async_computation.8 | async-start | bytes 12976128 | tf_op jit(solution)/shard_map/reduce_scatter | solution.py:264
  857.3 1054.2 %reduce-scatter.17.cloned.1.call-start = ((), (), s32[]{:S(2)}) async-start(), calls=%async_computation.12 | async-start | bytes 17301504 | tf_op jit(solution)/shard_map/reduce_scatter | solution.py:266
  872.0 1398.9 %reduce-scatter.19.cloned.1.call-start = ((), (), s32[]{:S(2)}) async-start(), calls=%async_computation.13 | async-start | bytes 17301504 | tf_op jit(solution)/shard_map/reduce_scatter | solution.py:266
  886.9 1743.6 %reduce-scatter.21.cloned.1.call-start = ((), (), s32[]{:S(2)}) async-start(), calls=%async_computation.14 | async-start | bytes 17301504 | tf_op jit(solution)/shard_map/reduce_scatter | solution.py:267
  901.3 2088.7 %reduce-scatter.23.cloned.1.call-start = ((), (), s32[]{:S(2)}) async-start(), calls=%async_computation.15 | async-start | bytes 17301504 | tf_op jit(solution)/shard_map/reduce_scatter | solution.py:267
  928.0 304.2 %copy-start.53 = (f32[2,32,1024]{2,1,0:T(8,128)S(1)}, f32[2,32,1024]{2,1,0:T(8,128)}, u32[]{:S(2)}) copy-start(f32[2,32,1024]{2,1,0:T(8,128)} %param.20) | copy-start | bytes 786436
  928.1 624.1 %copy-start.44 = (f32[2,32,3072]{2,1,0:T(8,128)S(1)}, f32[2,32,3072]{2,1,0:T(8,128)}, u32[]{:S(2)}) copy-start(f32[2,32,3072]{2,1,0:T(8,128)} %param.19) | copy-start | bytes 2359300
  1232.2 1038.8 %copy-start.41 = (f32[2,32,4096]{2,1,0:T(8,128)S(1)}, f32[2,32,4096]{2,1,0:T(8,128)}, u32[]{:S(2)}) copy-start(f32[2,32,4096]{2,1,0:T(8,128)} %param.21) | copy-start | bytes 3145732
  2271.0 719.0 %copy-start.43 = (f32[2,128,1024]{2,1,0:T(8,128)S(1)}, f32[2,128,1024]{2,1,0:T(8,128)}, u32[]{:S(2)}) copy-start(f32[2,128,1024]{2,1,0:T(8,128)} %param.22) | copy-start | bytes 3145732
  2271.0 719.0 %copy-start.52 = (f32[2,128,1024]{2,1,0:T(8,128)S(1)}, f32[2,128,1024]{2,1,0:T(8,128)}, u32[]{:S(2)}) copy-start(f32[2,128,1024]{2,1,0:T(8,128)} %param.27) | copy-start | bytes 3145732
  (117 other events, 3333.5 us)
Sparse Core Ops, SparseCore 0:
  11.5 72.4 all-gather.18
  87.6 55.0 all-gather.20
  146.2 76.1 all-gather.22
  225.8 75.8 all-gather.24
  305.0 68.0 all-gather.26
  376.5 54.9 all-gather.28
  435.1 76.2 all-gather.30
  514.9 75.9 all-gather.32
  821.9 119.7 all-reduce.7
  943.9 145.4 reduce-scatter.14
  1091.6 140.5 reduce-scatter.12
  1238.1 152.4 reduce-scatter.10
  1397.7 154.4 reduce-scatter.8
  1554.3 357.1 reduce-scatter.16
  1913.6 357.2 reduce-scatter.18
  2273.1 357.3 reduce-scatter.20
  2632.6 357.3 reduce-scatter.22
where the time goes:
time: 3010 us; the launch traced here: 3000 us
  waiting for transfers between devices  2390 us (79%)
  matrix products  323 us (11%)
  local copies, waits for them, and re-layouts  165 us (5%)
  other arithmetic  65.6 us (2%)
  blocking collectives  43 us (1%)
    reduce_scatter x2, waiting for transfers between devices, on_device(): lax.psum_scatter(terms[2], ('node', 'chip'), scatter_dimension=0, tiled=T...  715 us
    reduce_scatter x2, waiting for transfers between devices, on_device(): lax.psum_scatter(terms[3], ('node', 'chip'), scatter_dimension=0, tiled=T...  715 us
    reduce_scatter x2, waiting for transfers between devices, on_device(): lax.psum_scatter(terms[0], ('node', 'chip'), scatter_dimension=0, tiled=T...  318 us
    reduce_scatter x2, waiting for transfers between devices, on_device(): lax.psum_scatter(terms[1], ('node', 'chip'), scatter_dimension=0, tiled=T...  288 us
    all_gather x2, waiting for transfers between devices, fetch_forward(): lax.all_gather(mlp_in, ('node', 'chip'), axis=0, tiled=True)  147 us
    all_gather x2, waiting for transfers between devices, fetch_forward(): lax.all_gather(mlp_out, ('node', 'chip'), axis=0, tiled=True)  97.1 us
    all_gather x2, waiting for transfers between devices, fetch_forward(): lax.all_gather(attn_in, ('node', 'chip'), axis=0, tiled=True)  70.7 us
    dot_general x2, matrix products, forward_layer(): jnp.dot(normed_m_b, w_up, preferred_element_type=jnp.float32) + bias_u  61.7 us
  transfers between devices with their start and end apart: 17, of which 17 were waited for; matrix products, arithmetic and copies ran while one was open for 10% of the time, Pallas kernels for 0%

commit v1 on v0

--- a/solution.py
+++ b/solution.py
@@ -1,9 +1,343 @@
+import functools
 import math
 
 import jax
 import jax.numpy as jnp
 from jax import lax
+from jax.experimental import pallas as pl
+from jax.experimental.pallas import tpu as pltpu
 from jax.sharding import PartitionSpec as P
+
+MESH = pl.DeviceIdType.MESH
+ALL = slice(None)
+
+
+class Shape:
+    def __init__(self, mesh):
+        self.X = mesh.shape["node"] // 2
+        chips = mesh.shape["chip"]
+        self.Q = 2 ** ((chips.bit_length() - 1) // 2)
+        self.P = chips // self.Q
+        self.devices = mesh.shape["node"] * chips
+        self.grid = (self.X, 2, self.P, self.Q)
+
+
+class Place(Shape):
+    def __init__(self, shape):
+        self.__dict__.update(shape.__dict__)
+        node, chip = lax.axis_index("node"), lax.axis_index("chip")
+        self.x, self.c = node // 2, lax.rem(node, 2)
+        self.p, self.q = chip // self.Q, lax.rem(chip, self.Q)
+
+    def size(self, axis):
+        return {"x": self.X, "p": self.P, "q": self.Q, "c": 2}[axis]
+
+    def mine(self, axis):
+        return {"x": self.x, "p": self.p, "q": self.q, "c": self.c}[axis]
+
+    def off(self, axis, k):
+        n = self.size(axis)
+        return lax.rem(self.mine(axis) + (k % n), n)
+
+    def device(self, axis, k):
+        at = {"x": self.x, "p": self.p, "q": self.q, "c": self.c}
+        at[axis] = self.off(axis, k)
+        return (at["x"] * 2 + at["c"], at["p"] * self.Q + at["q"])
+
+    def peers(self):
+        return [(a, k) for a in ("p", "q", "x", "c") for k in range(1, self.size(a))]
+
+    def greet(self):
+        barrier = pltpu.get_barrier_semaphore()
+        peers = self.peers()
+        for axis, k in peers:
+            pl.semaphore_signal(barrier, inc=1, device_id=self.device(axis, k), device_id_type=MESH)
+        pl.semaphore_wait(barrier, len(peers))
+
+
+def gather_copies(shape):
+    return (shape.P - 1) + 2 * (shape.X - 1) + 2 * (shape.Q - 1) + 1
+
+
+class Gather:
+    def __init__(self, at, src, dst, cols, order, send, recv, local):
+        self.at, self.src, self.dst, self.cols, self.order = at, src, dst, cols, order
+        self.send, self.recv, self.local = send, recv, local
+        self.used = 0
+        self.started = []
+        self.arrivals = {}
+
+    def region(self, **fix):
+        at = self.at
+        pick = dict(x=at.x, p=at.p, q=at.q, c=at.c)
+        pick.update(fix)
+        return self.dst.at[pick["x"], pick["c"], pick["p"], pick["q"], :, self.cols]
+
+    def push(self, phase, axis, k, held, src=None):
+        at, slot = self.at, self.used
+        self.used += 1
+        out = self.region(**held)
+        if axis == "c":
+            came = self.region(**dict(held, c=1 - at.c))
+        else:
+            came = self.region(**dict(held, **{axis: at.off(axis, -k)}))
+        sems = dict(send_sem=self.send.at[slot], recv_sem=self.recv.at[slot])
+        copy = pltpu.make_async_remote_copy(
+            src_ref=out if src is None else src, dst_ref=out, device_id=at.device(axis, k), device_id_type=MESH, **sems)
+        copy.start()
+        self.started.append(copy)
+        arrive = pltpu.make_async_remote_copy(
+            src_ref=came, dst_ref=came, device_id=at.device(axis, k), device_id_type=MESH, **sems)
+        self.arrivals.setdefault(phase, []).append(arrive)
+
+    def settle(self, phase):
+        for copy in self.arrivals.pop(phase, []):
+            copy.wait_recv()
+
+    def step(self, phase):
+        at = self.at
+        second, third = self.order
+        if phase == 0:
+            own = self.src.at[:, self.cols]
+            self.keep = pltpu.make_async_copy(own, self.region(), self.local)
+            self.keep.start()
+            for k in range(1, at.P):
+                self.push(1, "p", k, {}, src=own)
+        elif phase == 1:
+            self.keep.wait()
+            self.settle(1)
+            for k in range(1, at.size(second)):
+                self.push(2, second, k, dict(p=ALL))
+            self.push(4, "c", 1, dict(p=ALL))
+        elif phase == 2:
+            self.settle(2)
+            for k in range(1, at.size(third)):
+                self.push(3, third, k, {"p": ALL, second: ALL})
+            for k in range(1, at.size(second)):
+                self.push(4, "c", 1, {"p": ALL, second: at.off(second, k)})
+        elif phase == 3:
+            self.settle(3)
+            for k in range(1, at.size(third)):
+                self.push(4, "c", 1, {"p": ALL, second: ALL, third: at.off(third, k)})
+        elif phase == 4:
+            self.settle(4)
+
+    def finish(self):
+        for copy in self.started:
+            copy.wait_send()
+
+
+def halves(width, parts):
+    piece = width // parts
+    return [
+        (pl.ds(i * piece, piece // 2), pl.ds(i * piece + piece // 2, piece // 2)) for i in range(parts)
+    ]
+
+
+def gather_kernel(shape, parts, *refs):
+    n = len(parts)
+    srcs, dsts = refs[:n], refs[n : 2 * n]
+    send, recv, local = refs[2 * n :]
+    at = Place(shape)
+    at.greet()
+    jobs = []
+    for src, dst, count in zip(srcs, dsts, parts):
+        for pair in halves(src.shape[1], count):
+            jobs.append([])
+            for cols, order in zip(pair, (("q", "x"), ("x", "q"))):
+                slot = 2 * (len(jobs) - 1) + len(jobs[-1])
+                jobs[-1].append(Gather(at, src, dst, cols, order, send.at[slot], recv.at[slot], local.at[slot]))
+    for step in range(len(jobs) + 4):
+        for phase in range(4, -1, -1):
+            if 0 <= step - phase < len(jobs):
+                for job in jobs[step - phase]:
+                    job.step(phase)
+    for pair in jobs:
+        for job in pair:
+            job.finish()
+
+
+def all_gather(shape, arrays, parts, collective_id):
+    count = 2 * sum(parts)
+    copies = gather_copies(shape)
+    return pl.pallas_call(
+        functools.partial(gather_kernel, shape, parts),
+        out_shape=[jax.ShapeDtypeStruct(shape.grid + a.shape, a.dtype) for a in arrays],
+        in_specs=[pl.BlockSpec(memory_space=pl.ANY)] * len(arrays),
+        out_specs=[pl.BlockSpec(memory_space=pl.ANY)] * len(arrays),
+        scratch_shapes=[
+            pltpu.SemaphoreType.DMA((count, copies)),
+            pltpu.SemaphoreType.DMA((count, copies)),
+            pltpu.SemaphoreType.DMA((count,)),
+        ],
+        compiler_params=pltpu.CompilerParams(
+            collective_id=collective_id, has_side_effects=True, vmem_limit_bytes=16 * 2**20),
+    )(*arrays)
+
+
+class Scatter:
+    def __init__(self, at, src, out, cols, order, acc, bufs, send, recv, local):
+        self.at, self.src, self.out, self.cols, self.order = at, src, out, cols, order
+        self.acc, self.bufs, self.send, self.recv, self.local = acc, bufs, send, recv, local
+        self.used = 0
+        self.started = []
+        self.waiting = []
+
+    def part(self, **fix):
+        return tuple(fix.get(a, ALL) for a in ("x", "p", "q"))
+
+    def push(self, axis, k, src, dst):
+        slot = self.used
+        self.used += 1
+        copy = pltpu.make_async_remote_copy(
+            src_ref=src, dst_ref=dst, send_sem=self.send.at[slot], recv_sem=self.recv.at[slot],
+            device_id=self.at.device(axis, k), device_id_type=MESH)
+        copy.start()
+        self.started.append(copy)
+        self.waiting.append(copy)
+
+    def settle(self):
+        for copy in self.waiting:
+            copy.wait_recv()
+        self.waiting = []
+
+    def add(self, index, terms):
+        total = self.acc[index]
+        for term in terms:
+            total = total + term
+        self.acc[index] = total
+
+    def step(self, phase):
+        at, acc = self.at, self.acc
+        first, second = self.order
+        b0, b1, b2, b3 = self.bufs
+        if phase == 0:
+            self.keep = pltpu.make_async_copy(self.src.at[:, at.c, :, :, :, self.cols], acc, self.local)
+            self.keep.start()
+            self.push("c", 1, self.src.at[:, 1 - at.c, :, :, :, self.cols], b0)
+        elif phase == 1:
+            self.keep.wait()
+            self.settle()
+            for i in range(at.X):
+                self.add(i, [b0[i]])
+            for k in range(1, at.size(first)):
+                self.push(first, k, acc.at[self.part(**{first: at.off(first, k)})], b1.at[k - 1])
+        elif phase == 2:
+            self.settle()
+            own = self.part(**{first: at.mine(first)})
+            self.add(own, [b1[k - 1] for k in range(1, at.size(first))])
+            for k in range(1, at.size(second)):
+                self.push(second, k, acc.at[self.part(**{first: at.mine(first), second: at.off(second, k)})], b2.at[k - 1])
+        elif phase == 3:
+            self.settle()
+            own = self.part(x=at.x, q=at.q)
+            self.add(own, [b2[k - 1] for k in range(1, at.size(second))])
+            for k in range(1, at.P):
+                self.push("p", k, acc.at[at.x, at.off("p", k), at.q], b3.at[k - 1])
+        elif phase == 4:
+            self.settle()
+            total = acc[at.x, at.p, at.q].astype(jnp.float32)
+            for k in range(1, at.P):
+                total = total + b3[k - 1].astype(jnp.float32)
+            self.out[:, self.cols] = total
+
+    def finish(self):
+        for copy in self.started:
+            copy.wait_send()
+
+
+def scatter_copies(shape):
+    return 1 + (shape.X - 1) + (shape.Q - 1) + (shape.P - 1)
+
+
+def scatter_buffers(shape, rows, width, order):
+    X, P, Q = shape.X, shape.P, shape.Q
+    block = (rows, width)
+    if order[0] == "x":
+        first = (X - 1, P, Q) + block
+        second = (Q - 1, P) + block
+    else:
+        first = (Q - 1, X, P) + block
+        second = (X - 1, P) + block
+    return [(X, P, Q) + block, (X, P, Q) + block, first, second, (P - 1,) + block]
+
+
+ORDERS = (("x", "q"), ("q", "x"))
+
+
+def scatter_kernel(shape, parts, *refs):
+    n = len(parts)
+    srcs, outs = refs[:n], refs[n : 2 * n]
+    count = 2 * sum(parts)
+    bufs = refs[2 * n : 2 * n + 5 * count]
+    send, recv, local = refs[2 * n + 5 * count :]
+    at = Place(shape)
+    at.greet()
+    jobs = []
+    for src, out, pieces in zip(srcs, outs, parts):
+        for pair in halves(src.shape[-1], pieces):
+            jobs.append([])
+            for cols, order in zip(pair, ORDERS):
+                slot = 2 * (len(jobs) - 1) + len(jobs[-1])
+                mine = bufs[5 * slot : 5 * slot + 5]
+                jobs[-1].append(
+                    Scatter(at, src, out, cols, order, mine[0], mine[1:], send.at[slot], recv.at[slot], local.at[slot]))
+    for step in range(len(jobs) + 4):
+        for phase in range(4, -1, -1):
+            if 0 <= step - phase < len(jobs):
+                for job in jobs[step - phase]:
+                    job.step(phase)
+    for pair in jobs:
+        for job in pair:
+            job.finish()
+
+
+def reduce_scatter(shape, arrays, parts, collective_id):
+    count, copies = 2 * sum(parts), scatter_copies(shape)
+    scratch = []
+    for a, pieces in zip(arrays, parts):
+        rows, cols = a.shape[-2:]
+        for _ in range(pieces):
+            for order in ORDERS:
+                scratch += [
+                    pltpu.VMEM(s, jnp.bfloat16) for s in scatter_buffers(shape, rows, cols // pieces // 2, order)
+                ]
+    return pl.pallas_call(
+        functools.partial(scatter_kernel, shape, parts),
+        out_shape=[jax.ShapeDtypeStruct(a.shape[-2:], jnp.float32) for a in arrays],
+        in_specs=[pl.BlockSpec(memory_space=pl.ANY)] * len(arrays),
+        out_specs=[pl.BlockSpec(memory_space=pltpu.VMEM)] * len(arrays),
+        scratch_shapes=scratch
+        + [
+            pltpu.SemaphoreType.DMA((count, copies)),
+            pltpu.SemaphoreType.DMA((count, copies)),
+            pltpu.SemaphoreType.DMA((count,)),
+        ],
+        compiler_params=pltpu.CompilerParams(
+            collective_id=collective_id, has_side_effects=True, vmem_limit_bytes=60 * 2**20),
+    )(*arrays)
+
+GATHER_PARTS = (3, 1, 2, 2)
+SCATTER_PARTS = (3, 1, 4, 4)
+SLAB = (16, 256)
+
+
+def pack_vectors(mine):
+    flat = mine.reshape(-1)
+    return jnp.pad(flat, (0, SLAB[0] * SLAB[1] - flat.size)).reshape(SLAB)
+
+
+def unpack_vectors(slabs, layers, entries):
+    flat = slabs.reshape(-1, SLAB[0] * SLAB[1])[:, : layers * entries]
+    return flat.reshape(-1, layers, entries).transpose(1, 0, 2).reshape(layers, -1)
+
+
+def spread_vectors(shape, terms):
+    layers, entries = terms.shape
+    flat = terms.reshape(layers, shape.devices, -1).transpose(1, 0, 2).reshape(shape.devices, -1)
+    flat = jnp.pad(flat, ((0, 0), (0, SLAB[0] * SLAB[1] - flat.shape[1])))
+    return flat.reshape(shape.grid + SLAB)
+
 
 D = 1024
 HEADS = 16
@@ -189,32 +523,6 @@
     return (d_hidden, (g_in, g_out, g_up, g_down, d_vector))
 
 
-def fetch_forward(shards, layer_index):
-    attn_in, attn_out, mlp_in, mlp_out, vector_row = [
-        member[layer_index].astype(jnp.bfloat16) for member in shards
-    ]
-    return (
-        lax.all_gather(attn_in, ("node", "chip"), axis=0, tiled=True),
-        lax.all_gather(attn_out, ("node", "chip"), axis=0, tiled=True),
-        lax.all_gather(mlp_in, ("node", "chip"), axis=0, tiled=True),
-        lax.all_gather(mlp_out, ("node", "chip"), axis=0, tiled=True),
-        lax.all_gather(vector_row, ("node", "chip"), axis=0, tiled=True),
-    )
-
-
-def fetch_backward(shards, layer_index):
-    attn_in, attn_out, mlp_in, mlp_out, vector_row = [
-        member[layer_index].astype(jnp.bfloat16) for member in shards
-    ]
-    return (
-        lax.all_gather(attn_in, ("node", "chip"), axis=0, tiled=True),
-        lax.all_gather(attn_out, ("node", "chip"), axis=0, tiled=True),
-        lax.all_gather(mlp_in, ("node", "chip"), axis=0, tiled=True),
-        lax.all_gather(mlp_out, ("node", "chip"), axis=0, tiled=True),
-        lax.all_gather(vector_row, ("node", "chip"), axis=0, tiled=True),
-    )
-
-
 def adamw(weight, gradient, first, second, rate, decay):
     first_new = beta_first * first + (1.0 - beta_first) * gradient
     second_new = beta_second * second + (1.0 - beta_second) * gradient * gradient
@@ -225,6 +533,7 @@
 
 
 def on_device(
+    shape,
     tokens,
     cotangent,
     w_attn_in,
@@ -246,31 +555,37 @@
     shards = (w_attn_in, w_attn_out, w_mlp_in, w_mlp_out, vectors)
     layers = w_attn_in.shape[0]
     token_rows = tokens.shape[0] * tokens.shape[1]
+    blocks = [shards[m][l].astype(jnp.bfloat16) for l in range(layers) for m in range(4)]
+    packed = pack_vectors(vectors.astype(jnp.bfloat16))
+    gathered = all_gather(shape, [packed] + blocks, (1,) + GATHER_PARTS * layers, 1)
+    vector_rows = unpack_vectors(gathered[0], layers, vectors.shape[1]).astype(jnp.float32)
+    weights = [
+        [w.reshape(-1, w.shape[-1]) for w in gathered[1 + 4 * l : 5 + 4 * l]] for l in range(layers)
+    ]
     hidden = tokens.astype(jnp.float32).reshape(token_rows, D)
     kept_values = []
     for layer_index in range(layers):
-        gathered = fetch_forward(shards, layer_index)
-        hidden, saved = forward_layer(hidden, gathered[:4], gathered[4].astype(jnp.float32))
+        hidden, saved = forward_layer(hidden, weights[layer_index], vector_rows[layer_index])
         kept_values.append(saved)
     output = hidden.reshape(tokens.shape).astype(jnp.bfloat16)
     upstream = cotangent.astype(jnp.float32).reshape(token_rows, D)
     collected = [None] * layers
+    vector_terms = [None] * layers
     for layer_index in reversed(range(layers)):
-        gathered = fetch_backward(shards, layer_index)
         upstream, terms = backward_layer(
-            upstream, kept_values[layer_index], gathered[:4], gathered[4].astype(jnp.float32)
+            upstream, kept_values[layer_index], weights[layer_index], vector_rows[layer_index]
         )
-        collected[layer_index] = (
-            lax.psum_scatter(terms[0], ("node", "chip"), scatter_dimension=0, tiled=True),
-            lax.psum_scatter(terms[1], ("node", "chip"), scatter_dimension=0, tiled=True),
-            lax.psum_scatter(terms[2], ("node", "chip"), scatter_dimension=0, tiled=True),
-            lax.psum_scatter(terms[3], ("node", "chip"), scatter_dimension=0, tiled=True),
-            lax.psum_scatter(terms[4], ("node", "chip"), scatter_dimension=0, tiled=True),
-        )
-    stacked = [
-        jnp.stack([collected[layer_index][member] for layer_index in range(layers)])
-        for member in range(5)
-    ]
+        vector_terms[layer_index] = terms[4]
+        blocks = [
+            t.astype(jnp.bfloat16).reshape(shape.grid + (t.shape[0] // shape.devices, t.shape[1])) for t in terms[:4]
+        ]
+        parts = SCATTER_PARTS
+        if layer_index == 0:
+            blocks = blocks + [spread_vectors(shape, jnp.stack(vector_terms).astype(jnp.bfloat16))]
+            parts = parts + (1,)
+        collected[layer_index] = reduce_scatter(shape, blocks, parts, 2 + layer_index)
+    stacked = [jnp.stack([collected[l][member] for l in range(layers)]) for member in range(4)]
+    stacked.append(collected[0][4].reshape(-1)[: vectors.size].reshape(vectors.shape))
     firsts = (first_attn_in, first_attn_out, first_mlp_in, first_mlp_out, first_vectors)
     seconds = (second_attn_in, second_attn_out, second_mlp_in, second_mlp_out, second_vectors)
     settings = (
@@ -353,5 +668,5 @@
         P(None, ("node", "chip")),
     )
     return jax.shard_map(
-        on_device, mesh=mesh, in_specs=in_specs, out_specs=out_specs, check_vma=False
-    )
+        functools.partial(on_device, Shape(mesh)), mesh=mesh, in_specs=in_specs, out_specs=out_specs, check_vma=False
+    )

time: 3010 us -> 1080 us (0.36)
  waiting for transfers between devices: 2390 us -> 0 us
  Pallas kernels: 0 us -> 515 us
  blocking collectives: 43 us -> 0 us
    reduce_scatter x8 -> x0, waiting for transfers between devices: 2040 us -> none  [the longest x2 715 us: on_device(): lax.psum_scatter(terms[2], ('node', 'chip'), scatter_dimension=0, tiled=T...]
    pallas_call x0 -> x3, Pallas kernels: none -> 515 us  [the longest x2 271 us: reduce_scatter(): pl.pallas_call(functools.partial(scatter_kernel, shape, parts), out_shape...]
    all_gather x8 -> x0, waiting for transfers between devices: 338 us -> none  [the longest x2 147 us: fetch_forward(): lax.all_gather(mlp_in, ('node', 'chip'), axis=0, tiled=True)]
    unnamed x1 -> x0, blocking collectives: 43 us -> none
  transfers between devices with their start and end apart: 17 -> 0, of which waited for: 17 -> 0; matrix products, arithmetic and copies ran while one was open for 10% -> 0% of each run, Pallas kernels for 0% -> 0%
where the time goes in v1:
time: 1080 us; the launch traced here: 1070 us
  Pallas kernels  515 us (48%)
  matrix products  315 us (29%)
  local copies, waits for them, and re-layouts  175 us (16%)
  other arithmetic  63.4 us (6%)
    pallas_call x2, Pallas kernels, reduce_scatter(): pl.pallas_call(functools.partial(scatter_kernel, shape, parts), out_shape...  271 us
    pallas_call x1, Pallas kernels, all_gather(): pl.pallas_call(functools.partial(gather_kernel, shape, parts), out_shape=...  244 us
    dot_general x2, matrix products, forward_layer(): jnp.dot(normed_m_b, w_up, preferred_element_type=jnp.float32) + bias_u  61.4 us
    unnamed x317, local copies, waits for them, and re-layouts  34.2 us
    dot_general x2, matrix products, backward_layer(): jnp.einsum('td,fd->tf', d_down_b, w_down, preferred_element_type=jnp.floa...  27.5 us
    dot_general x2, matrix products, backward_layer(): jnp.einsum('td,tf->df', normed_m_b, d_upper_b, preferred_element_type=jnp...  24.5 us
    convert_element_type x2, other arithmetic, backward_layer(): d_scores_b = d_scores.astype(jnp.bfloat16)  23.4 us

profile of v1, /device:TPU:0, one launch (start us, length us, event | category | flops | bytes accessed | tf_op | source)
XLA Modules:
  0.0 1071.1 jit_solution(9471800042237533103)
XLA Ops:
  3.7 244.1 %shard_map.296 = (bf16[2,2,4,2,16,256]{5,4,3,2,1,0:T(8,128)(2,1)S(1)}, bf16[2,2,4,2,32,3072]{5,4,3,2,1,0:T(8,128)(2,1)S(1)}, bf16[2,2,4,2,32,1024]{5,4,3,2,1,0:T...) custom-call(bf16[16,256]{1,0:T(8,128)(2,1)S(1)} %reshape.395.refs_0_, ...), custom_call_target="tpu_custom_call" | custom-call | tf_op jit(solution)/shard_map/pallas_call | solution.py:163
  307.6 7.1 convert_bitcast_fusion.1
  334.3 30.1 %fusion.2 = (bf16[580,4096]{1,0:T(8,128)(2,1)S(1)}, f32[580,4096]{1,0:T(8,128)}) fusion(f32[4096]{0:T(1024)S(1)} %bitcast.235, bf16[1024,4096]{1,0:T(8,128)(2,1)} %bitcast.164, f32[580,1024]{1,0:T(8,128)S(1)} %get-tuple-element.183, f32[1024]{0:T(1024)S(1)} %bitcast.255, f32[1024]{0:T(1024)S(1)} %bitcast.218, f32[580]{0:T(1024)S(1)} %add_rsqrt_fusion.3, ...), kind=kOutput, calls=%fused_computation.16 | convolution fusion | flops 5025157120 | bytes 25047584 | tf_op jit(solution)/shard_map/dot_general | solution.py:414
  426.8 31.3 %fusion.5 = (bf16[580,4096]{1,0:T(8,128)(2,1)}, f32[580,4096]{1,0:T(8,128)}) fusion(f32[4096]{0:T(1024)S(1)} %bitcast.237, bf16[1024,4096]{1,0:T(8,128)(2,1)} %bitcast.262, f32[580,1024]{1,0:T(8,128)S(1)} %get-tuple-element.179, f32[1024]{0:T(1024)S(1)} %bitcast.249, f32[1024]{0:T(1024)S(1)} %bitcast.251, f32[580]{0:T(1024)S(1)} %add_rsqrt_fusion.1, ...), kind=kOutput, calls=%fused_computation.19 | convolution fusion | flops 5025157120 | bytes 25047584 | tf_op jit(solution)/shard_map/dot_general | solution.py:414
  461.2 12.9 %fusion.82 = (bf16[4096]{0:T(1024)(128)(2,1)}, bf16[580,4096]{1,0:T(8,128)(2,1)S(1)}) fusion(f32[580,4096]{1,0:T(8,128)} %get-tuple-element.238, f32[4096]{0:T(1024)S(1)} %bitcast.238, bf16[580,1024]{1,0:T(8,128)(2,1)} %convert_element_type.214, bf16[4096,1024]{1,0:T(8,128)(2,1)} %bitcast.260), kind=kOutput, calls=%fused_computation.255 | convolution fusion | flops 4893896704 | bytes 23855104 | tf_op jit(solution)/shard_map/td,fd->tf/dot_general | solution.py:465
  474.1 11.9 %multiply_reduce_fusion.5 = (bf16[1024]{0:T(1024)(128)(2,1)}, f32[580]{0:T(1024)S(1)}, f32[580]{0:T(1024)S(1)}, bf16[1024]{0:T(1024)(128)(2,1)}, f32[580,1024]{1,0:T(8,128)}) fusion(f32[580,1024]{1,0:T(8,128)S(1)} %copy-done.40, f32[580]{0:T(1024)S(1)} %add_rsqrt_fusion.1, f32[580]{0:T(1024)S(1)} %broadcast_multiply_fusion.9, f32[1024]{0:T(1024)S(1)} %bitcast.252, ...), kind=kOutput, calls=%fused_computation.94 | convolution fusion | flops 4870734848 | bytes 17908800 | tf_op jit(solution)/shard_map/tf,df->td/dot_general | solution.py:472
  491.3 14.5 %multiply_reduce_fusion.4 = (bf16[1024]{0:T(1024)(128)(2,1)S(1)}, bf16[580,1024]{1,0:T(8,128)(2,1)}, bf16[1024]{0:T(1024)(128)(2,1)S(1)}, bf16[1024]{0:T(1024)(128)(2,1)S(1)}, f32[580,1024]{1,0:T(8,128)S(1)}) fusion(f32[580,1024]{1,0:T(8,128)} %reshape.411, f32[1024]{0:T(1024)S(1)} %bitcast.257, f32[580,1024]{1,0:T(8,128)} %copy-done.39, ...), kind=kOutput, calls=%fused_computation.93 | convolution fusion | flops 4876674048 | bytes 26242112 | tf_op jit(solution)/shard_map/dot_general | solution.py:416
  515.8 7.8 bitcast_convert_fusion.2
  530.6 9.2 multiply_reduce_fusion.1
  539.8 11.7 %multiply_convert_fusion.1 = bf16[4,16,145,145]{2,3,1,0:T(8,128)(2,1)} fusion(f32[4,16,145,145]{2,3,1,0:T(8,128)} %get-tuple-element.241, f32[4,16,145,145]{2,3,1,0:T(8,128)} %copy-done.10, f32[4,16,145]{2,1,0:T(8,128)S(1)} %get-tuple-element.240, f32[4,16,145]{2,1,0:T(8,128)S(1)} %log_add_fusion), kind=kLoop, calls=%fused_computation.6 | loop fusion | flops 6728000 | bytes 13530240 | tf_op jit(solution)/shard_map/convert_element_type | solution.py:490
  587.4 14.6 %fusion.83 = (bf16[4096]{0:T(1024)(128)(2,1)S(1)}, bf16[580,4096]{1,0:T(8,128)(2,1)}) fusion(f32[580,4096]{1,0:T(8,128)} %get-tuple-element.232, f32[4096]{0:T(1024)S(1)} %bitcast.236, bf16[4096,1024]{1,0:T(8,128)(2,1)} %bitcast.168, f32[580,1024]{1,0:T(8,128)S(1)} %get-tuple-element.175, f32[1024]{0:T(1024)S(1)} %bitcast.224), kind=kOutput, calls=%fused_computation.256 | convolution fusion | flops 4895084544 | bytes 25047040 | tf_op jit(solution)/shard_map/td,fd->tf/dot_general | solution.py:465
  602.1 8.4 multiply_reduce_fusion.9
  622.1 7.8 bitcast_convert_fusion
  637.6 9.0 multiply_reduce_fusion
  646.7 11.7 %multiply_convert_fusion = bf16[4,16,145,145]{2,3,1,0:T(8,128)(2,1)} fusion(f32[4,16,145,145]{2,3,1,0:T(8,128)} %get-tuple-element.249, f32[4,16,145,145]{2,3,1,0:T(8,128)} %copy-done.9, f32[4,16,145]{2,1,0:T(8,128)S(1)} %get-tuple-element.248, f32[4,16,145]{2,1,0:T(8,128)S(1)} %log_add_fusion.1), kind=kLoop, calls=%fused_computation.4 | loop fusion | flops 6728000 | bytes 13530240 | tf_op jit(solution)/shard_map/convert_element_type | solution.py:490
  686.6 10.3 multiply_reduce_fusion.11
  706.6 12.0 %convolution_convert_fusion.3 = bf16[4096,1024]{1,0:T(8,128)(2,1)} fusion(bf16[580,4096]{1,0:T(8,128)(2,1)} %copy-done.132, f32[580,1024]{1,0:T(8,128)} %copy-done.28, f32[1024]{0:T(1024)S(1)} %bitcast.225), kind=kOutput, calls=%fused_computation.67 | convolution fusion | flops 4870774784 | bytes 15519744 | tf_op jit(solution)/shard_map/tf,td->fd/dot_general | solution.py:464
  718.7 12.3 %convolution_convert_fusion.1 = bf16[1024,4096]{1,0:T(8,128)(2,1)} fusion(bf16[580,4096]{1,0:T(8,128)(2,1)} %get-tuple-element.258, f32[580,1024]{1,0:T(8,128)S(1)} %copy-done.25, f32[1024]{0:T(1024)S(1)} %bitcast.256, f32[1024]{0:T(1024)S(1)} %bitcast.221, f32[580]{0:T(1024)S(1)} %copy-done.101, f32[580]{0:T(1024)S(1)} %copy-done.81), kind=kOutput, calls=%fused_computation.65 | convolution fusion | flops 4872556544 | bytes 15528480 | tf_op jit(solution)/shard_map/td,tf->df/dot_general | solution.py:471
  734.1 9.8 convolution_convert_fusion.5
  744.0 140.1 %shard_map.297 = (f32[32,3072]{1,0:T(8,128)}, f32[32,1024]{1,0:T(8,128)}, f32[32,4096]{1,0:T(8,128)}, f32[128,1024]{1,0:T(8,128)}, f32[16,256]{1,0:T(8,128)}) custom-call(bf16[2,2,4,2,32,3072]{5,4,3,2,1,0:T(8,128)(2,1)} %bitcast.189, bf16[2,2,4,2,32,1024]{5,4,3,2,1,0:T(8,128)(2,1)} %bitcast.191, bf16[2,2,4,2,32,4096]{5,4,3,2,1,0:T(8,128)(2,1)} %bitcast.186, ...), custom_call_target="tpu_custom_call" | custom-call | tf_op jit(solution)/shard_map/pallas_call | solution.py:305
  884.2 12.2 %convolution_convert_fusion = bf16[1024,4096]{1,0:T(8,128)(2,1)} fusion(bf16[580,4096]{1,0:T(8,128)(2,1)} %copy-done.131, f32[580,1024]{1,0:T(8,128)} %copy-done.39, f32[1024]{0:T(1024)S(1)} %bitcast.250, f32[1024]{0:T(1024)S(1)} %bitcast.254, f32[580]{0:T(1024)S(1)} %copy-done.128, f32[580]{0:T(1024)S(1)} %copy-done.103), kind=kOutput, calls=%fused_computation.64 | convolution fusion | flops 4872556544 | bytes 15528480 | tf_op jit(solution)/shard_map/td,tf->df/dot_general | solution.py:471
  899.6 8.2 convolution_convert_fusion.4
  907.9 9.0 convolution_convert_fusion.2
  916.9 130.6 %shard_map.298 = (f32[32,3072]{1,0:T(8,128)}, f32[32,1024]{1,0:T(8,128)}, f32[32,4096]{1,0:T(8,128)}, f32[128,1024]{1,0:T(8,128)}) custom-call(bf16[2,2,4,2,32,3072]{5,4,3,2,1,0:T(8,128)(2,1)} %bitcast.188, bf16[2,2,4,2,32,1024]{5,4,3,2,1,0:T(8,128)(2,1)} %bitcast.190, bf16[2,2,4,2,32,4096]{5,4,3,2,1,0:T(8,128)(2,1)} %bitcast.184, ...), custom_call_target="tpu_custom_call" | custom-call | tf_op jit(solution)/shard_map/pallas_call | solution.py:305
  (460 shorter events, 291.2 us)
Async XLA Ops:
  3.4 260.7 %copy-start.17 = (bf16[4,145,1024]{2,0,1:T(4,128)(2,1)S(1)}, bf16[4,145,1024]{2,0,1:T(4,128)(2,1)}, u32[]{:S(2)}) copy-start(bf16[4,145,1024]{2,0,1:T(4,128)(2,1)} %param.17) | copy-start | bytes 3563524
  263.4 64.5 %copy-start.92 = (f32[1,1024]{1,0:T(1,128)}, f32[1,1024]{1,0:T(1,128)S(1)}, u32[]{:S(2)}) copy-start(f32[1,1024]{1,0:T(1,128)S(1)} %get-tuple-element.219) | copy-start | bytes 12292
  263.4 70.8 %copy-start.88 = (f32[1,1024]{1,0:T(1,128)}, f32[1,1024]{1,0:T(1,128)S(1)}, u32[]{:S(2)}) copy-start(f32[1,1024]{1,0:T(1,128)S(1)} %get-tuple-element.217) | copy-start | bytes 12292
  263.4 70.8 %copy-start.123 = (f32[1,1024]{1,0:T(1,128)}, f32[1,1024]{1,0:T(1,128)S(1)}, u32[]{:S(2)}) copy-start(f32[1,1024]{1,0:T(1,128)S(1)} %get-tuple-element.216) | copy-start | bytes 12292
  263.5 101.0 %copy-start.90 = (f32[1,1024]{1,0:T(1,128)}, f32[1,1024]{1,0:T(1,128)S(1)}, u32[]{:S(2)}) copy-start(f32[1,1024]{1,0:T(1,128)S(1)} %get-tuple-element.218) | copy-start | bytes 12292
  263.5 101.0 %copy-start.94 = (f32[1,1024]{1,0:T(1,128)}, f32[1,1024]{1,0:T(1,128)S(1)}, u32[]{:S(2)}) copy-start(f32[1,1024]{1,0:T(1,128)S(1)} %get-tuple-element.215) | copy-start | bytes 12292
  263.5 108.2 %copy-start.84 = (f32[1,1024]{1,0:T(1,128)}, f32[1,1024]{1,0:T(1,128)S(1)}, u32[]{:S(2)}) copy-start(f32[1,1024]{1,0:T(1,128)S(1)} %get-tuple-element.213) | copy-start | bytes 12292
  263.5 108.2 %copy-start.115 = (f32[1,1024]{1,0:T(1,128)}, f32[1,1024]{1,0:T(1,128)S(1)}, u32[]{:S(2)}) copy-start(f32[1,1024]{1,0:T(1,128)S(1)} %get-tuple-element.212) | copy-start | bytes 12292
  328.0 36.5 %slice-start.2 = ((s8[8388608]{0:T(1024)(128)(4,1)}), s8[4194304]{0:T(1024)(128)(4,1)S(1)}, s32[]{:S(2)}) async-start(s8[8388608]{0:T(1024)(128)(4,1)} %bitcast.169), calls=%async_computation.2 | async-start | bytes 8388608
  328.0 43.7 %slice-start.4 = ((s8[6291456]{0:T(1024)(128)(4,1)}), s8[4194304]{0:T(1024)(128)(4,1)S(1)}, s32[]{:S(2)}) async-start(s8[6291456]{0:T(1024)(128)(4,1)} %bitcast.174), calls=%async_computation.4 | async-start | bytes 8388608
  332.9 31.6 %copy-start.23 = (f32[580,1024]{1,0:T(8,128)}, f32[580,1024]{1,0:T(8,128)S(1)}, u32[]{:S(2)}) copy-start(f32[580,1024]{1,0:T(8,128)S(1)} %get-tuple-element.183) | copy-start | bytes 7127044
  332.9 31.6 %copy-start.80 = (f32[580]{0:T(1024)}, f32[580]{0:T(1024)S(1)}, u32[]{:S(2)}) copy-start(f32[580]{0:T(1024)S(1)} %broadcast_multiply_fusion.11) | copy-start | bytes 6964
  334.3 37.4 %slice-start.5 = ((s8[6291456]{0:T(1024)(128)(4,1)}), s8[2097152]{0:T(1024)(128)(4,1)S(1)}, s32[]{:S(2)}) async-start(s8[6291456]{0:T(1024)(128)(4,1)} %bitcast.174), calls=%async_computation.5 | async-start | bytes 4194304
  426.3 31.7 %copy-start.39 = (f32[580,1024]{1,0:T(8,128)}, f32[580,1024]{1,0:T(8,128)S(1)}, u32[]{:S(2)}) copy-start(f32[580,1024]{1,0:T(8,128)S(1)} %get-tuple-element.179) | copy-start | bytes 7127044
  426.3 65.0 %copy-start.102 = (f32[580]{0:T(1024)}, f32[580]{0:T(1024)S(1)}, u32[]{:S(2)}) copy-start(f32[580]{0:T(1024)S(1)} %broadcast_multiply_fusion.9) | copy-start | bytes 6964
  426.7 64.6 %copy-start.127 = (f32[580]{0:T(1024)}, f32[580]{0:T(1024)S(1)}, u32[]{:S(2)}) copy-start(f32[580]{0:T(1024)S(1)} %add_rsqrt_fusion.1) | copy-start | bytes 6964
  426.8 31.3 %copy-start.32 = (bf16[4,145,1024]{2,0,1:T(4,128)(2,1)S(1)}, bf16[4,145,1024]{2,0,1:T(4,128)(2,1)}, u32[]{:S(2)}) copy-start(bf16[4,145,1024]{2,0,1:T(4,128)(2,1)} %param.18) | copy-start | bytes 3563524
  426.8 31.3 %copy-start.82 = (f32[1,1024]{1,0:T(1,128)S(1)}, f32[1,1024]{1,0:T(1,128)}, u32[]{:S(2)}) copy-start(f32[1,1024]{1,0:T(1,128)} %get-tuple-element.205) | copy-start | bytes 12292
  744.0 140.2 %copy-start.103 = (f32[580]{0:T(1024)S(1)}, f32[580]{0:T(1024)}, u32[]{:S(2)}) copy-start(f32[580]{0:T(1024)} %copy-done.102) | copy-start | bytes 6964
  744.0 140.2 %copy-start.120 = (f32[1,1024]{1,0:T(1,128)S(1)}, f32[1,1024]{1,0:T(1,128)}, u32[]{:S(2)}) copy-start(f32[1,1024]{1,0:T(1,128)} %get-tuple-element.207) | copy-start | bytes 12292
  744.0 140.1 %copy-start.122 = (f32[1,1024]{1,0:T(1,128)S(1)}, f32[1,1024]{1,0:T(1,128)}, u32[]{:S(2)}) copy-start(f32[1,1024]{1,0:T(1,128)} %get-tuple-element.208) | copy-start | bytes 12292
  744.0 140.1 %copy-start.128 = (f32[580]{0:T(1024)S(1)}, f32[580]{0:T(1024)}, u32[]{:S(2)}) copy-start(f32[580]{0:T(1024)} %copy-done.127) | copy-start | bytes 6964
  916.9 130.7 %copy-start.34 = (f32[2,128,1024]{2,1,0:T(8,128)S(1)}, f32[2,128,1024]{2,1,0:T(8,128)}, u32[]{:S(2)}) copy-start(f32[2,128,1024]{2,1,0:T(8,128)} %param.22) | copy-start | bytes 3145732
  916.9 130.7 %copy-start.63 = (f32[128,1024]{1,0:T(8,128)S(1)}, f32[128,1024]{1,0:T(8,128)}, u32[]{:S(2)}) copy-start(f32[128,1024]{1,0:T(8,128)} %get-tuple-element.50) | copy-start | bytes 1572868
  (119 other events, 817.5 us)

commit v2 on v0

v2 whole, which is shorter than its diff:
```python
import functools
import math

import jax
import jax.numpy as jnp
from jax import lax
from jax.experimental import pallas as pl
from jax.experimental.pallas import tpu as pltpu
from jax.sharding import PartitionSpec as P

STEP = 10
beta_first = 0.9
beta_second = 0.999
adam_eps = 1e-08
SLAB = (16, 256)
MESH = pl.DeviceIdType.MESH
ALL = slice(None)
D = 1024
HEADS = 16
HEAD_DIM = 64
FF = 4096
SEQ = 145
SPAN = 160
GROUP = 256
FF_TILE = 512
ROWS = 16
norm_eps = 1e-06
LOW = jnp.bfloat16
FULL = jnp.float32
GAIN_A, SHIFT_A, BIAS_Q, BIAS_V, BIAS_O, SCALE_A, GAIN_M, SHIFT_M, BIAS_D, SCALE_M, BIAS_U = range(11)


class Shape:
    def __init__(self, mesh):
        chips = mesh.shape["chip"]
        self.X = mesh.shape["node"] // 2
        self.Q = 2 ** ((chips.bit_length() - 1) // 2)
        self.P = chips // self.Q
        self.devices = mesh.shape["node"] * chips
        self.grid = (self.X, 2, self.P, self.Q)
        self.sizes = {"x": self.X, "c": 2, "p": self.P, "q": self.Q}


class Place:
    def __init__(self, shape):
        self.sizes = shape.sizes
        node, chip = lax.axis_index("node"), lax.axis_index("chip")
        self.at = {"x": node // 2, "c": lax.rem(node, 2), "p": chip // shape.Q, "q": lax.rem(chip, shape.Q)}
        self.offs, self.devices = {}, {}
        for axis, n in shape.sizes.items():
            for k in range(1, n):
                off = lax.rem(self.at[axis] + k, n)
                to = dict(self.at, **{axis: off})
                self.offs[axis, k] = off
                self.devices[axis, k] = (to["x"] * 2 + to["c"], to["p"] * shape.Q + to["q"])

    def off(self, axis, k):
        return self.offs[axis, k % self.sizes[axis]]

    def greet(self):
        barrier = pltpu.get_barrier_semaphore()
        for device in self.devices.values():
            pl.semaphore_signal(barrier, inc=1, device_id=device, device_id_type=MESH)
        pl.semaphore_wait(barrier, len(self.devices))


class Move:
    def __init__(self, src, dst, came, sems, device):
        if device is None:
            copy = functools.partial(pltpu.make_async_copy, src, dst, sems[0])
            self.start, self.arrived, self.sent = lambda: copy().start(), lambda: copy().wait(), None
        else:
            copy = functools.partial(
                pltpu.make_async_remote_copy,
                send_sem=sems[0], recv_sem=sems[1], device_id=device, device_id_type=MESH)
            self.start = lambda: copy(src, dst).start()
            self.sent = lambda: copy(src, dst).wait_send()
            self.arrived = lambda: copy(came, came).wait_recv()


class Task:
    def __init__(self, place, sems):
        self.place, self.sems, self.used = place, sems, 0
        self.phases = [([], [], []) for _ in range(5)]

    def move(self, begin, end, src, dst, came=None, axis=None, k=None):
        slot, self.used = self.used, self.used + 1
        sems = (self.sems[0].at[slot], self.sems[1].at[slot])
        move = Move(src, dst, dst if came is None else came, sems, None if axis is None else self.place.devices[axis, k])
        self.phases[begin][2].append(move)
        self.phases[end][0].append(move)


class Pipeline:
    def __init__(self, place, jobs):
        self.place, self.jobs = place, jobs

    def plan(self, steps):
        flying, unsent, todo = [], [], {}
        for step in steps:
            acts = todo[step] = []
            for phase in range(4, -1, -1):
                if not 0 <= step - phase < len(self.jobs):
                    continue
                for task in self.jobs[step - phase]:
                    waits, work, starts = task.phases[phase]
                    acts += [move.arrived for move in waits if move in flying]
                    flying = [move for move in flying if move not in waits] + starts
                    acts += work + [move.start for move in starts]
                    unsent += [move.sent for move in starts if move.sent is not None]
        return todo, [move.arrived for move in flying] + unsent


class Gather(Task):
    def __init__(self, place, src, dst, cols, order, sems):
        super().__init__(place, sems)
        at, sizes = place.at, place.sizes
        second, third = order

        def region(**fix):
            pick = dict(at, **fix)
            return dst.at[pick["x"], pick["c"], pick["p"], pick["q"], :, cols]

        def push(begin, end, axis, k, own=None, **held):
            came = region(**dict(held, **{axis: place.off(axis, -k)}))
            self.move(begin, end, region(**held) if own is None else own, region(**held), came, axis, k)

        if src is not None:
            own = src.at[:, cols]
            self.move(0, 1, own, region())
            for k in range(1, sizes["p"]):
                push(0, 1, "p", k, own)
        for k in range(1, sizes[second]):
            push(1, 2, second, k, p=ALL)
        push(1, 4, "c", 1, p=ALL)
        for k in range(1, sizes[third]):
            push(2, 3, third, k, **{"p": ALL, second: ALL})
        for k in range(1, sizes[second]):
            push(2, 4, "c", 1, **{"p": ALL, second: place.off(second, k)})
        for k in range(1, sizes[third]):
            push(3, 4, "c", 1, **{"p": ALL, second: ALL, third: place.off(third, k)})


class Scatter(Task):
    def __init__(self, place, src, out, cols, order, bufs, sems):
        super().__init__(place, sems)
        at, sizes = place.at, place.sizes
        first, second = order
        acc, b0, b1, b2, b3 = bufs

        def part(**fix):
            return tuple(fix.get(a, ALL) for a in ("x", "p", "q"))

        def add(index, terms):
            total = acc[index]
            for term in terms:
                total = total + term[...]
            acc[index] = total

        def finish():
            total = acc[at["x"], at["p"], at["q"]].astype(FULL)
            for k in range(1, sizes["p"]):
                total = total + b3[k - 1].astype(FULL)
            out[:, cols] = total

        self.move(0, 1, src.at[:, at["c"], :, :, :, cols], acc)
        self.move(0, 1, src.at[:, place.off("c", 1), :, :, :, cols], b0, None, "c", 1)
        for i in range(sizes["x"]):
            self.phases[1][1].append(functools.partial(add, i, [b0.at[i]]))
        for k in range(1, sizes[first]):
            self.move(1, 2, acc.at[part(**{first: place.off(first, k)})], b1.at[k - 1], None, first, k)
        self.phases[2][1].append(
            functools.partial(add, part(**{first: at[first]}), [b1.at[k - 1] for k in range(1, sizes[first])]))
        for k in range(1, sizes[second]):
            away = part(**{first: at[first], second: place.off(second, k)})
            self.move(2, 3, acc.at[away], b2.at[k - 1], None, second, k)
        self.phases[3][1].append(
            functools.partial(add, part(x=at["x"], q=at["q"]), [b2.at[k - 1] for k in range(1, sizes[second])]))
        for k in range(1, sizes["p"]):
            self.move(3, 4, acc.at[at["x"], place.off("p", k), at["q"]], b3.at[k - 1], None, "p", k)
        self.phases[4][1].append(finish)


def halves(width, piece, pieces):
    size = width // pieces // 2
    return [pl.ds((2 * piece + i) * size, size) for i in range(2)]


ANYWHERE = pl.BlockSpec(memory_space=pl.ANY)


class Gathering:
    def __init__(self, shape, sources, jobs, first, last, held):
        self.shape, self.jobs, self.steps, self.held = shape, jobs, list(range(first, last)), held
        active = [i for i in range(len(jobs)) if i < last and i + 4 >= first]
        self.active = active
        self.fresh = sorted({m for i in active if i >= first for m, _, _ in jobs[i]})
        self.names = sorted({m for i in active for m, _, _ in jobs[i]})
        under_way = [m for m in self.names if m in held]
        self.inputs = [sources[m] for m in self.fresh] + [held[m] for m in under_way]
        self.in_specs = [ANYWHERE] * len(self.inputs)
        self.out_shape = [jax.ShapeDtypeStruct(shape.grid + sources[m].shape, LOW) for m in self.names]
        self.out_specs = [ANYWHERE] * len(self.names)
        self.aliases = {len(self.fresh) + i: self.names.index(m) for i, m in enumerate(under_way)}
        tasks = sum(2 * len(jobs[i]) for i in active)
        sizes = shape.sizes
        copies = sizes["p"] + 2 * (sizes["x"] - 1) + 2 * (sizes["q"] - 1) + 1
        self.scratch = [pltpu.SemaphoreType.DMA((tasks, copies))] * 2

    def build(self, ins, outs, scratch):
        place = Place(self.shape)
        send, recv = scratch
        made, slot = [], 0
        for i, job in enumerate(self.jobs):
            made.append([])
            if i not in self.active:
                continue
            for name, piece, pieces in job:
                dst = outs[self.names.index(name)]
                src = ins[self.fresh.index(name)] if i >= self.steps[0] else None
                for cols, order in zip(halves(dst.shape[-1], piece, pieces), (("q", "x"), ("x", "q"))):
                    made[-1].append(Gather(place, src, dst, cols, order, (send.at[slot], recv.at[slot])))
                    slot += 1
        return Pipeline(place, made)

    def take(self, outs):
        self.held.update(zip(self.names, outs))


class Scattering:
    def __init__(self, shape, arrays, pieces):
        self.shape, self.pieces = shape, pieces
        self.inputs, self.in_specs = list(arrays), [ANYWHERE] * len(arrays)
        self.steps = list(range(sum(pieces) + 4))
        self.out_shape = [jax.ShapeDtypeStruct(a.shape[-2:], FULL) for a in arrays]
        self.out_specs = [whole(a.shape[-2:]) for a in arrays]
        self.aliases = {}
        X, P_, Q = shape.X, shape.P, shape.Q
        self.scratch = []
        for a, n in zip(arrays, pieces):
            block = (a.shape[-2], a.shape[-1] // n // 2)
            for _ in range(n):
                for one in (((X - 1, P_, Q), (Q - 1, P_)), ((Q - 1, X, P_), (X - 1, P_))):
                    for lead in ((X, P_, Q), (X, P_, Q)) + one + ((P_ - 1,),):
                        self.scratch.append(pltpu.VMEM(lead + block, LOW))
        tasks = 2 * sum(pieces)
        copies = 2 + (X - 1) + (Q - 1) + (P_ - 1)
        self.scratch += [pltpu.SemaphoreType.DMA((tasks, copies))] * 2

    def build(self, ins, outs, scratch):
        place = Place(self.shape)
        send, recv = scratch[-2:]
        made, slot = [], 0
        for src, out, n in zip(ins, outs, self.pieces):
            for piece in range(n):
                made.append([])
                for cols, order in zip(halves(src.shape[-1], piece, n), (("x", "q"), ("q", "x"))):
                    bufs = scratch[5 * slot : 5 * slot + 5]
                    made[-1].append(Scatter(place, src, out, cols, order, bufs, (send.at[slot], recv.at[slot])))
                    slot += 1
        return Pipeline(place, made)

    def take(self, outs):
        self.sums = outs


def beside(kernel, points, transfer, pace, number, grid, inputs, in_specs, out_specs, out_shape, scratch, name, limit=60):
    total = grid * points
    when = {}
    if transfer is not None:
        for i, step in enumerate(transfer.steps):
            when.setdefault(min(total, i * total // pace), []).append(step)
    counts = [len(inputs), len(transfer.inputs) if transfer else 0, len(out_shape), len(transfer.out_shape) if transfer else 0, len(scratch)]

    def body(*refs):
        groups, i = [], 0
        for n in counts:
            groups.append(refs[i : i + n])
            i += n
        groups.append(refs[i:])
        step = pl.program_id(0)
        if transfer is None:
            kernel(lambda point: None, *groups[0], *groups[2], *groups[4])
            return
        pipe = transfer.build(groups[1], groups[3], groups[5])
        todo, rest = pipe.plan(transfer.steps)

        def tick(point):
            for time in sorted(when):
                if time < total and time % points == point:
                    @pl.when(step == time // points)
                    def _():
                        if time == 0:
                            pipe.place.greet()
                        for act in [act for s in when[time] for act in todo[s]]:
                            act()

        kernel(tick, *groups[0], *groups[2], *groups[4])

        @pl.when(step == grid - 1)
        def _():
            for act in [act for s in when.get(total, []) for act in todo[s]] + rest:
                act()

    extra = {}
    if transfer is not None:
        extra["input_output_aliases"] = {counts[0] + i: counts[2] + o for i, o in transfer.aliases.items()}
        inputs, in_specs = list(inputs) + transfer.inputs, list(in_specs) + transfer.in_specs
        out_specs, out_shape = list(out_specs) + transfer.out_specs, list(out_shape) + transfer.out_shape
        scratch = list(scratch) + transfer.scratch
    outs = pl.pallas_call(
        body,
        grid=(grid,),
        in_specs=in_specs,
        out_specs=out_specs,
        out_shape=out_shape,
        scratch_shapes=scratch,
        name=name,
        compiler_params=pltpu.CompilerParams(
            dimension_semantics=("arbitrary",),
            vmem_limit_bytes=limit * 2**20,
            collective_id=None if transfer is None else number,
            has_side_effects=transfer is not None,
        ),
        **extra,
    )(*inputs)
    if transfer is not None:
        transfer.take(outs[counts[2] :])
    return outs[: counts[2]]


def mul(a, b):
    return jnp.dot(a, b, preferred_element_type=FULL)


def mul_nt(a, b):
    return lax.dot_general(a, b, (((1,), (1,)), ((), ())), preferred_element_type=FULL)


def mul_tn(a, b):
    return lax.dot_general(a, b, (((0,), (0,)), ((), ())), preferred_element_type=FULL)


def normalise(values):
    centred = values - jnp.mean(values, axis=-1, keepdims=True)
    inverse = lax.rsqrt(jnp.mean(centred * centred, axis=-1, keepdims=True) + norm_eps)
    return centred * inverse, inverse


def tiles(rows, step=160):
    return [slice(i, i + step) for i in range(0, rows, step)]


def row(vec, index):
    return vec[index : index + 1, :]


def softmax_of(q, k, lanes, width):
    scores = mul_nt(jnp.where(lanes, q, jnp.zeros_like(q)), k) * HEAD_DIM ** (-0.5)
    scores = jnp.where(width, scores, -1e30)
    expo = jnp.exp(scores - jnp.max(scores, axis=-1, keepdims=True))
    return expo * (1.0 / jnp.sum(expo, axis=-1, keepdims=True))


def lane_sets():
    lane = lax.broadcasted_iota(jnp.int32, (SPAN, 128), 1)
    return [lane < HEAD_DIM, lane >= HEAD_DIM]


def key_set():
    return lax.broadcasted_iota(jnp.int32, (SPAN, SPAN), 1) < SEQ


def attend_fwd(tick, h, vec, wq, wk, wv, wo, a_out, q_out, k_out, v_out, mixed_out, branch_out, mid_out, mixed, total):
    step, last = pl.program_id(0), pl.num_programs(0) - 1
    rows = h.shape[0]
    tick(0)

    @pl.when(step == 0)
    def _():
        for t in tiles(rows):
            normal, _ = normalise(h[t, :])
            a_out[t, :] = (normal * row(vec, GAIN_A) + row(vec, SHIFT_A)).astype(LOW)
        total[...] = jnp.zeros_like(total)

    group = pl.ds(pl.multiple_of(step * GROUP, GROUP), GROUP)
    q_out[...] = (mul(a_out[...], wq[...]) + vec[BIAS_Q : BIAS_Q + 1, group]).astype(LOW)
    k_out[...] = mul(a_out[...], wk[...]).astype(LOW)
    v_out[...] = (mul(a_out[...], wv[...]) + vec[BIAS_V : BIAS_V + 1, group]).astype(LOW)
    tick(1)
    lanes, width = lane_sets(), key_set()

    def image(i, carry):
        at = pl.ds(pl.multiple_of(i * SPAN, SPAN), SPAN)
        for pair in range(GROUP // 128):
            cols = slice(pair * 128, pair * 128 + 128)
            q, k, v = q_out[at, cols], k_out[at, cols], v_out[at, cols]
            both = [mul(softmax_of(q, k, lanes[s], width).astype(LOW), v) for s in range(2)]
            mixed[at, cols] = jnp.where(lanes[0], both[0], both[1]).astype(LOW)
        return carry

    images = rows // SPAN
    lax.fori_loop(0, images // 2, image, 0)
    tick(2)
    lax.fori_loop(images // 2, images, image, 0)
    mixed_out[...] = mixed[...]
    total[...] += mul(mixed[...], wo[...])

    @pl.when(step == last)
    def _():
        for t in tiles(rows):
            branch = total[t, :] + row(vec, BIAS_O)
            branch_out[t, :] = branch
            mid_out[t, :] = h[t, :] + row(vec, SCALE_A) * branch


def whole(shape):
    return pl.BlockSpec(shape, lambda j: (0,) * len(shape), pipeline_mode=pl.Buffered(1))


def columns(rows, width, at=0):
    return pl.BlockSpec((rows, width), lambda j: (0, j + at))


def lines(height, cols):
    return pl.BlockSpec((height, cols), lambda j: (j, 0))


def attention_forward(h, vec, w_in, w_out, transfer=None, pace=1, number=0):
    rows = h.shape[0]
    n = D // GROUP
    f32, low = lambda s: jax.ShapeDtypeStruct(s, FULL), lambda s: jax.ShapeDtypeStruct(s, LOW)
    full = whole((rows, D))
    cols = columns(rows, GROUP)
    return beside(
        attend_fwd,
        points=3,
        transfer=transfer,
        pace=pace,
        number=number,
        grid=n,
        inputs=[h, vec, w_in, w_in, w_in, w_out],
        in_specs=[full, whole(vec.shape)]
        + [columns(D, GROUP, i * n) for i in range(3)]
        + [lines(GROUP, D)],
        out_specs=[full, cols, cols, cols, cols, full, full],
        out_shape=[low((rows, D))] * 5 + [f32((rows, D))] * 2,
        scratch=[pltpu.VMEM((rows, GROUP), LOW), pltpu.VMEM((rows, D), FULL)],
        name="attention_forward",
    )


def phi_of(u):
    return 0.5 * (1.0 + lax.erf(u * 0.5**0.5))


def mlp_fwd(tick, mid, vec, wu, wd, c_out, u_out, act_out, down_out, next_out, low_out, total):
    step, last = pl.program_id(0), pl.num_programs(0) - 1
    rows = mid.shape[0]
    tick(0)

    @pl.when(step == 0)
    def _():
        for t in tiles(rows):
            normal, _ = normalise(mid[t, :])
            c_out[t, :] = (normal * row(vec, GAIN_M) + row(vec, SHIFT_M)).astype(LOW)
        total[...] = jnp.zeros_like(total)

    per = D // FF_TILE
    bias = vec[pl.ds(BIAS_U + step // per, 1), pl.ds(pl.multiple_of(lax.rem(step, per) * FF_TILE, FF_TILE), FF_TILE)]

    def part(i, carry):
        t = pl.ds(pl.multiple_of(i * SPAN, SPAN), SPAN)
        u = mul(c_out[t, :], wu[...]) + bias
        u_out[t, :] = u
        act = (u * phi_of(u)).astype(LOW)
        act_out[t, :] = act
        total[t, :] += mul(act, wd[...])
        return carry

    images = rows // SPAN
    lax.fori_loop(0, images // 2, part, 0)
    tick(1)
    lax.fori_loop(images // 2, images, part, 0)

    @pl.when(step == last)
    def _():
        for t in tiles(rows):
            down = total[t, :] + row(vec, BIAS_D)
            down_out[t, :] = down
            result = mid[t, :] + row(vec, SCALE_M) * down
            next_out[t, :] = result
            low_out[t, :] = result.astype(LOW)


def mlp_forward(mid, vec, w_up, w_down, transfer=None, pace=1, number=0):
    rows = mid.shape[0]
    f32, low = lambda s: jax.ShapeDtypeStruct(s, FULL), lambda s: jax.ShapeDtypeStruct(s, LOW)
    full = whole((rows, D))
    tile = columns(rows, FF_TILE)
    return beside(
        mlp_fwd,
        points=2,
        transfer=transfer,
        pace=pace,
        number=number,
        grid=FF // FF_TILE,
        inputs=[mid, vec, w_up, w_down],
        in_specs=[full, whole(vec.shape), columns(D, FF_TILE), lines(FF_TILE, D)],
        out_specs=[full, tile, tile, full, full, full],
        out_shape=[low((rows, D)), f32((rows, FF)), low((rows, FF)), f32((rows, D)), f32((rows, D)), low((rows, D))],
        scratch=[pltpu.VMEM((rows, D), FULL)],
        name="mlp_forward",
    )


def norm_back(values, upstream, gain):
    normal, inverse = normalise(values)
    scaled = upstream * gain
    inner = (
        scaled
        - jnp.mean(scaled, axis=-1, keepdims=True)
        - normal * jnp.mean(scaled * normal, axis=-1, keepdims=True)
    )
    return inverse * inner, upstream * normal


def summed(values):
    return jnp.sum(values, axis=0, keepdims=True)


def mlp_bwd(tick, g, down, mid, branch, c, vec, u, act, wu, wd, g_down, g_up, d_mid, db_out, sums, d_bias_u, dd, total):
    step, last = pl.program_id(0), pl.num_programs(0) - 1
    rows = g.shape[0]
    tick(0)

    @pl.when(step == 0)
    def _():
        sums[...] = jnp.zeros_like(sums)
        for t in tiles(rows):
            grad = g[t, :]
            scaled = grad * row(vec, SCALE_M)
            sums[SCALE_M : SCALE_M + 1, :] += summed(grad * down[t, :])
            sums[BIAS_D : BIAS_D + 1, :] += summed(scaled)
            dd[t, :] = scaled.astype(LOW)
        total[...] = jnp.zeros_like(total)

    g_down[...] = mul_tn(act[...], dd[...]).astype(LOW)
    tick(1)
    d_act = mul_nt(dd[...], wd[...])
    upper = u[...]
    density = jnp.exp(-0.5 * upper * upper) * (2.0 * math.pi) ** (-0.5)
    du = d_act * (phi_of(upper) + upper * density)
    d_bias_u[...] = summed(du)
    du_b = du.astype(LOW)
    tick(2)
    g_up[...] = mul_tn(c[...], du_b).astype(LOW)
    total[...] += mul_nt(du_b, wu[...])

    @pl.when(step == last)
    def _():
        for t in tiles(rows):
            upstream = total[t, :]
            through, gain_terms = norm_back(mid[t, :], upstream, row(vec, GAIN_M))
            sums[GAIN_M : GAIN_M + 1, :] += summed(gain_terms)
            sums[SHIFT_M : SHIFT_M + 1, :] += summed(upstream)
            middle = g[t, :] + through
            d_mid[t, :] = middle
            sums[SCALE_A : SCALE_A + 1, :] += summed(middle * branch[t, :])
            db = middle * row(vec, SCALE_A)
            sums[BIAS_O : BIAS_O + 1, :] += summed(db)
            db_out[t, :] = db.astype(LOW)


def mlp_backward(g, down, mid, branch, c, vec, u, act, w_up, w_down, transfer=None, pace=1, number=0):
    rows = g.shape[0]
    f32, low = lambda s: jax.ShapeDtypeStruct(s, FULL), lambda s: jax.ShapeDtypeStruct(s, LOW)
    full = whole((rows, D))
    tile = columns(rows, FF_TILE)
    return beside(
        mlp_bwd,
        points=3,
        transfer=transfer,
        pace=pace,
        number=number,
        grid=FF // FF_TILE,
        inputs=[g, down, mid, branch, c, vec, u, act, w_up, w_down],
        in_specs=[full] * 5 + [whole(vec.shape), tile, tile, columns(D, FF_TILE), lines(FF_TILE, D)],
        out_specs=[lines(FF_TILE, D), columns(D, FF_TILE), full, full, whole((ROWS, D)), columns(1, FF_TILE)],
        out_shape=[low((FF, D)), low((D, FF)), f32((rows, D)), low((rows, D)), f32((ROWS, D)), f32((1, FF))],
        scratch=[pltpu.VMEM((rows, D), LOW), pltpu.VMEM((rows, D), FULL)],
        name="mlp_backward",
    )


def attend_bwd(tick, d_mid, db, h, a, vec, q, k, v, mixed, wq, wk, wv, wo, gq, gk, gv, go, g_out, sums, d_bias, dq, dk, dv, dm, total):
    step, last = pl.program_id(0), pl.num_programs(0) - 1
    rows = h.shape[0]
    tick(0)

    @pl.when(step == 0)
    def _():
        sums[...] = jnp.zeros_like(sums)
        total[...] = jnp.zeros_like(total)

    dm[...] = mul_nt(db[...], wo[...]).astype(LOW)
    go[...] = mul_tn(mixed[...], db[...]).astype(LOW)
    tick(1)
    lanes, width = lane_sets(), key_set()
    d_bias[...] = jnp.zeros_like(d_bias)

    def image(i, carry):
        at = pl.ds(pl.multiple_of(i * SPAN, SPAN), SPAN)
        for pair in range(GROUP // 128):
            cols = slice(pair * 128, pair * 128 + 128)
            qp, kp, vp, dmp = q[at, cols], k[at, cols], v[at, cols], dm[at, cols]
            grads = []
            for s in range(2):
                prob = softmax_of(qp, kp, lanes[s], width)
                d_prob = mul_nt(jnp.where(lanes[s], dmp, jnp.zeros_like(dmp)), vp)
                ds = (prob * (d_prob - jnp.sum(prob * d_prob, axis=-1, keepdims=True))).astype(LOW)
                grads.append((mul(ds, kp), mul_tn(ds, qp), mul_tn(prob.astype(LOW), dmp)))
            d_q, d_k, d_v = [jnp.where(lanes[0], one, two) for one, two in zip(*grads)]
            d_q, d_k = d_q * HEAD_DIM ** (-0.5), d_k * HEAD_DIM ** (-0.5)
            dq[at, cols], dk[at, cols], dv[at, cols] = d_q.astype(LOW), d_k.astype(LOW), d_v.astype(LOW)
            d_bias[0:1, cols] += summed(d_q)
            d_bias[1:2, cols] += summed(d_v)
        return carry

    images = rows // SPAN
    lax.fori_loop(0, images // 2, image, 0)
    tick(2)
    lax.fori_loop(images // 2, images, image, 0)
    tick(3)
    gq[...] = mul_tn(a[...], dq[...]).astype(LOW)
    gk[...] = mul_tn(a[...], dk[...]).astype(LOW)
    gv[...] = mul_tn(a[...], dv[...]).astype(LOW)
    total[...] += mul_nt(dq[...], wq[...]) + mul_nt(dk[...], wk[...]) + mul_nt(dv[...], wv[...])

    @pl.when(step == last)
    def _():
        for t in tiles(rows):
            upstream = total[t, :]
            through, gain_terms = norm_back(h[t, :], upstream, row(vec, GAIN_A))
            sums[GAIN_A : GAIN_A + 1, :] += summed(gain_terms)
            sums[SHIFT_A : SHIFT_A + 1, :] += summed(upstream)
            g_out[t, :] = d_mid[t, :] + through


def attention_backward(d_mid, db, h, a, vec, q, k, v, mixed, w_in, w_out, transfer=None, pace=1, number=0):
    rows = h.shape[0]
    n = D // GROUP
    f32, low = lambda s: jax.ShapeDtypeStruct(s, FULL), lambda s: jax.ShapeDtypeStruct(s, LOW)
    full = whole((rows, D))
    cols = columns(rows, GROUP)
    weight = columns(D, GROUP)
    return beside(
        attend_bwd,
        points=4,
        transfer=transfer,
        pace=pace,
        number=number,
        grid=n,
        inputs=[d_mid, db, h, a, vec, q, k, v, mixed, w_in, w_in, w_in, w_out],
        in_specs=[full] * 4
        + [whole(vec.shape)]
        + [cols] * 4
        + [columns(D, GROUP, i * n) for i in range(3)]
        + [lines(GROUP, D)],
        out_specs=[weight] * 3 + [lines(GROUP, D), full, whole((ROWS, D)), columns(8, GROUP)],
        out_shape=[low((D, D))] * 4 + [f32((rows, D)), f32((ROWS, D)), f32((8, D))],
        scratch=[pltpu.VMEM((rows, GROUP), LOW)] * 4 + [pltpu.VMEM((rows, D), FULL)],
        name="attention_backward",
    )


GATHER_PIECES = (3, 1, 2, 2)
GATHER_CUTS = (0, 8, 12, 16, 20)
GATHER_PACE = (2, 3, 3, 1)
SCATTER_PIECES = (4, 4)
SCATTER_PACE = (8, 12)


def transfer_alone(transfer, number, name):
    beside(lambda tick: tick(0), 1, transfer, len(transfer.steps), number, 1, [], [], [], [], [], name)


def shape_blocks(shape, term):
    return term.reshape(shape.grid + (term.shape[0] // shape.devices, term.shape[1]))


def spread_rows(tokens):
    return jnp.pad(tokens, ((0, 0), (0, SPAN - SEQ), (0, 0))).reshape(-1, D)


def pack_vectors(mine):
    flat = mine.reshape(-1)
    return jnp.pad(flat, (0, SLAB[0] * SLAB[1] - flat.size)).reshape(SLAB)


def unpack_vectors(slabs, layers, entries):
    flat = slabs.reshape(-1, SLAB[0] * SLAB[1])[:, : layers * entries]
    return flat.reshape(-1, layers, entries).transpose(1, 0, 2).reshape(layers, -1)


def spread_vectors(shape, terms):
    layers, entries = terms.shape
    flat = terms.reshape(layers, shape.devices, -1).transpose(1, 0, 2).reshape(shape.devices, -1)
    flat = jnp.pad(flat, ((0, 0), (0, SLAB[0] * SLAB[1] - flat.shape[1])))
    return flat.reshape(shape.grid + SLAB)


D = 1024
HEADS = 16
HEAD_DIM = 64
FF = 4096
STEP = 10
SEQ = 145


def adamw(weight, gradient, first, second, rate, decay):
    first_new = beta_first * first + (1.0 - beta_first) * gradient
    second_new = beta_second * second + (1.0 - beta_second) * gradient * gradient
    fix_first = 1.0 - beta_first**STEP
    fix_second = 1.0 - beta_second**STEP
    stepped = first_new / fix_first / (jnp.sqrt(second_new / fix_second) + adam_eps)
    return (weight - rate * (stepped + decay * weight), first_new, second_new)


def on_device(
    shape,
    tokens,
    cotangent,
    w_attn_in,
    w_attn_out,
    w_mlp_in,
    w_mlp_out,
    vectors,
    first_attn_in,
    first_attn_out,
    first_mlp_in,
    first_mlp_out,
    first_vectors,
    second_attn_in,
    second_attn_out,
    second_mlp_in,
    second_mlp_out,
    second_vectors,
):
    shards = (w_attn_in, w_attn_out, w_mlp_in, w_mlp_out, vectors)
    layers, images = w_attn_in.shape[0], tokens.shape[0]
    sources = [pack_vectors(vectors.astype(LOW))]
    jobs = []
    for layer in range(layers):
        sources += [shards[m][layer].astype(LOW) for m in range(4)]
        jobs += [[(1 + 4 * layer + m, piece, n)] for m, n in enumerate(GATHER_PIECES) for piece in range(n)]
    jobs[0].append((0, 0, 1))
    held = {}
    cuts = GATHER_CUTS

    def matrix(name):
        return held[name].reshape(-1, held[name].shape[-1])

    def gathering(index):
        return Gathering(shape, sources, jobs, cuts[index], cuts[index + 1], held)

    transfer_alone(gathering(0), 1, "gather")
    rows_of = unpack_vectors(held[0], layers, vectors.shape[1]).astype(FULL).reshape(layers, -1, D)
    hidden = spread_rows(tokens.astype(FULL))
    kept = []
    for layer in range(layers):
        vec, base = rows_of[layer], 1 + 4 * layer
        transfer = gathering(1 + 2 * layer)
        w_in, w_out = matrix(base), matrix(base + 1)
        a, q, k, v, mixed, branch, mid = attention_forward(
            hidden, vec, w_in, w_out, transfer=transfer, pace=GATHER_PACE[2 * layer], number=2 + 2 * layer)
        transfer = gathering(2 + 2 * layer) if layer < layers - 1 else None
        w_up, w_down = matrix(base + 2), matrix(base + 3)
        c, u, act, down, result, low = mlp_forward(
            mid, vec, w_up, w_down, transfer=transfer, pace=GATHER_PACE[2 * layer + 1], number=3 + 2 * layer)
        kept.append((vec, w_in, w_out, w_up, w_down, hidden, a, q, k, v, mixed, branch, mid, c, u, act, down))
        hidden = result
    output = low.reshape(images, SPAN, D)[:, :SEQ]
    grad = spread_rows(cotangent.astype(FULL))
    terms, sums = [None] * layers, [[None] * 6 for _ in range(layers)]
    waiting, number = None, 10
    for layer in reversed(range(layers)):
        vec, w_in, w_out, w_up, w_down, hidden, a, q, k, v, mixed, branch, mid, c, u, act, down = kept[layer]
        transfer = None if waiting is None else Scattering(shape, waiting, (1, 1, 1, 1))
        g_down, g_up, d_mid, db, sums_m, d_bias_u = mlp_backward(
            grad, down, mid, branch, c, vec, u, act, w_up, w_down, transfer=transfer, pace=SCATTER_PACE[0], number=number)
        if transfer is not None:
            sums[layer + 1][:4] = transfer.sums
        transfer = Scattering(shape, [shape_blocks(shape, g) for g in (g_up, g_down)], SCATTER_PIECES)
        g_q, g_k, g_v, g_out, grad, sums_a, d_bias = attention_backward(
            d_mid, db, hidden, a, vec, q, k, v, mixed, w_in, w_out, transfer=transfer, pace=SCATTER_PACE[1], number=number + 1)
        sums[layer][4:] = transfer.sums
        waiting = [shape_blocks(shape, g) for g in (g_q, g_k, g_v, g_out)]
        number += 2
        both = sums_m + sums_a
        terms[layer] = jnp.concatenate(
            [both[:BIAS_Q].reshape(-1), d_bias[:2].reshape(-1), both[BIAS_O:BIAS_U].reshape(-1), d_bias_u.reshape(-1)])
    transfer = Scattering(shape, waiting + [spread_vectors(shape, jnp.stack(terms).astype(LOW))], (1, 1, 1, 1, 1))
    transfer_alone(transfer, number, "scatter")
    sums[0][:4] = transfer.sums[:4]
    stacked = [
        jnp.stack([jnp.concatenate(sums[layer][:3], axis=1) for layer in range(layers)]),
        jnp.stack([sums[layer][3] for layer in range(layers)]),
        jnp.stack([sums[layer][4] for layer in range(layers)]),
        jnp.stack([sums[layer][5] for layer in range(layers)]),
        transfer.sums[4].reshape(-1)[: vectors.size].reshape(vectors.shape),
    ]
    firsts = (first_attn_in, first_attn_out, first_mlp_in, first_mlp_out, first_vectors)
    seconds = (second_attn_in, second_attn_out, second_mlp_in, second_mlp_out, second_vectors)
    settings = (
        (D ** (-0.5), 0.05),
        ((D // 8) ** (-0.5), 0.05),
        (D ** (-0.5), 0.05),
        (FF ** (-0.5), 0.05),
        (0.3, 0.0),
    )
    updated = [
        adamw(
            shards[member],
            stacked[member],
            firsts[member],
            seconds[member],
            settings[member][0],
            settings[member][1],
        )
        for member in range(5)
    ]
    d_tokens = grad.reshape(images, SPAN, D)[:, :SEQ]
    return (
        output,
        d_tokens,
        updated[0][0],
        updated[1][0],
        updated[2][0],
        updated[3][0],
        updated[4][0],
        updated[0][1],
        updated[1][1],
        updated[2][1],
        updated[3][1],
        updated[4][1],
        updated[0][2],
        updated[1][2],
        updated[2][2],
        updated[3][2],
        updated[4][2],
    )


def solution(mesh):
    in_specs = (
        P(("node", "chip"), None, None),
        P(("node", "chip"), None, None),
        P(None, ("node", "chip"), None),
        P(None, ("node", "chip"), None),
        P(None, ("node", "chip"), None),
        P(None, ("node", "chip"), None),
        P(None, ("node", "chip")),
        P(None, ("node", "chip"), None),
        P(None, ("node", "chip"), None),
        P(None, ("node", "chip"), None),
        P(None, ("node", "chip"), None),
        P(None, ("node", "chip")),
        P(None, ("node", "chip"), None),
        P(None, ("node", "chip"), None),
        P(None, ("node", "chip"), None),
        P(None, ("node", "chip"), None),
        P(None, ("node", "chip")),
    )
    out_specs = (
        P(("node", "chip"), None, None),
        P(("node", "chip"), None, None),
        P(None, ("node", "chip"), None),
        P(None, ("node", "chip"), None),
        P(None, ("node", "chip"), None),
        P(None, ("node", "chip"), None),
        P(None, ("node", "chip")),
        P(None, ("node", "chip"), None),
        P(None, ("node", "chip"), None),
        P(None, ("node", "chip"), None),
        P(None, ("node", "chip"), None),
        P(None, ("node", "chip")),
        P(None, ("node", "chip"), None),
        P(None, ("node", "chip"), None),
        P(None, ("node", "chip"), None),
        P(None, ("node", "chip"), None),
        P(None, ("node", "chip")),
    )
    return jax.shard_map(
        functools.partial(on_device, Shape(mesh)), mesh=mesh, in_specs=in_specs, out_specs=out_specs, check_vma=False
    )
```

time: 3010 us -> 746 us (0.25)
  waiting for transfers between devices: 2390 us -> 0 us
  Pallas kernels: 0 us -> 685 us
  matrix products: 323 us -> 0 us
  local copies, waits for them, and re-layouts: 165 us -> 34.5 us
  other arithmetic: 65.6 us -> 19.6 us
  blocking collectives: 43 us -> 0 us
    reduce_scatter x8 -> x0, waiting for transfers between devices: 2040 us -> none  [the longest x2 715 us: on_device(): lax.psum_scatter(terms[2], ('node', 'chip'), scatter_dimension=0, tiled=T...]
    pallas_call x0 -> x10, Pallas kernels: none -> 685 us  [beside(): pl.pallas_call(body, grid=(grid,), in_specs=in_specs, out_specs=out_specs...]
    all_gather x8 -> x0, waiting for transfers between devices: 338 us -> none  [the longest x2 147 us: fetch_forward(): lax.all_gather(mlp_in, ('node', 'chip'), axis=0, tiled=True)]
    dot_general x36 -> x0, matrix products: 323 us -> none  [the longest x2 61.7 us: forward_layer(): jnp.dot(normed_m_b, w_up, preferred_element_type=jnp.float32) + bias_u]
    reshape x25 -> x10, local copies, waits for them, and re-layouts: 93.3 us -> 9.79 us  [the longest x2 6.16 us: spread_rows(): return jnp.pad(tokens, ((0, 0), (0, SPAN - SEQ), (0, 0))).reshape(-1, D)]
    unnamed x1 -> x0, blocking collectives: 43 us -> none
  transfers between devices with their start and end apart: 17 -> 0, of which waited for: 17 -> 0; matrix products, arithmetic and copies ran while one was open for 10% -> 0% of each run, Pallas kernels for 0% -> 0%
where the time goes in v2:
time: 746 us; the launch traced here: 740 us
  Pallas kernels  685 us (92%)
  local copies, waits for them, and re-layouts  34.5 us (5%)
  other arithmetic  19.6 us (3%)
    pallas_call x10, Pallas kernels, beside(): pl.pallas_call(body, grid=(grid,), in_specs=in_specs, out_specs=out_specs...  685 us

profile of v2, /device:TPU:0, one launch (start us, length us, event | category | flops | bytes accessed | tf_op | source)
XLA Modules:
  0.0 740.1 jit_solution(6981422155137454675)
XLA Ops:
  0.7 2.0 pad_convert_fusion.1
  2.7 3.2 copy.48
  9.9 92.6 %gather.1 = (bf16[2,2,4,2,16,256]{5,4,3,2,1,0:T(8,128)(2,1)}, bf16[2,2,4,2,32,3072]{5,4,3,2,1,0:T(8,128)(2,1)}, bf16[2,2,4,2,32,1024]{5,4,3,2,1,0:T(8,128)(2,1)}...) custom-call(bf16[16,256]{1,0:T(8,128)(2,1)} %reshape.195.refs_0_, ...), custom_call_target="tpu_custom_call" | custom-call | tf_op jit(solution)/shard_map/gather/pallas_call | solution.py:311
  104.8 65.9 %attention_forward.2 = (bf16[640,1024]{1,0:T(8,128)(2,1)}, bf16[640,1024]{1,0:T(8,128)(2,1)}, bf16[640,1024]{1,0:T(8,128)(2,1)}, bf16[640,1024]{1,0:T(8,128)(2,1...) custom-call(f32[640,1024]{1,0:T(8,128)} %bitcast.97, ...), custom_call_target="tpu_custom_call", output_to_operand_aliasing={{7}: (8, {}), {8}: (9, {})} | custom-call | tf_op jit(solution)/shard_map/attention_forward/pallas_call | solution.py:311
  170.7 67.7 %mlp_forward.2 = (bf16[640,1024]{1,0:T(8,128)(2,1)}, f32[640,4096]{1,0:T(8,128)}, bf16[640,4096]{1,0:T(8,128)(2,1)}, f32[640,1024]{1,0:T(8,128)}, f32[640,1024]{...) custom-call(f32[640,1024]{1,0:T(8,128)} %get-tuple-element.100.refs_, ...), custom_call_target="tpu_custom_call", output_to_operand_aliasing={{6}: (6, {}), {7}: (7, {})} | custom-call | tf_op jit(solution)/shard_map/mlp_forward/pallas_call | solution.py:311
  239.2 48.7 %attention_forward.3 = (bf16[640,1024]{1,0:T(8,128)(2,1)}, bf16[640,1024]{1,0:T(8,128)(2,1)}, bf16[640,1024]{1,0:T(8,128)(2,1)}, bf16[640,1024]{1,0:T(8,128)(2,1...) custom-call(f32[640,1024]{1,0:T(8,128)} %get-tuple-element.105.refs_, ...), custom_call_target="tpu_custom_call", output_to_operand_aliasing={{7}: (6, {}), {8}: (7, {})} | custom-call | tf_op jit(solution)/shard_map/attention_forward/pallas_call | solution.py:311
  287.9 29.4 %mlp_forward.3 = (bf16[640,1024]{1,0:T(8,128)(2,1)}, f32[640,4096]{1,0:T(8,128)}, bf16[640,4096]{1,0:T(8,128)(2,1)}, f32[640,1024]{1,0:T(8,128)}, f32[640,1024]{1,0:T(8,128)}, /*index=5*/bf16[640,1024]{1,0:T(8,128)(2,1)}) custom-call(f32[640,1024]{1,0:T(8,128)} %get-tuple-element.110.refs_0_.refs_2_, f32[14,1024]{1,0:T(8,128)} %squeeze.5.refs_1_.refs_5_.refs_4_, ...), custom_call_target="tpu_custom_call" | custom-call | tf_op jit(solution)/shard_map/mlp_forward/pallas_call | solution.py:311
  317.3 1.5 slice.109
  318.8 1.9 copy.53
  321.5 3.0 copy.50
  324.4 41.4 %mlp_backward.2 = (bf16[4096,1024]{1,0:T(8,128)(2,1)}, bf16[1024,4096]{1,0:T(8,128)(2,1)}, f32[640,1024]{1,0:T(8,128)}, bf16[640,1024]{1,0:T(8,128)(2,1)}, f32[16,1024]{1,0:T(8,128)}, /*index=5*/f32[1,4096]{1,0:T(1,128)}) custom-call(f32[640,1024]{1,0:T(8,128)} %bitcast.101, f32[640,1024]{1,0:T(8,128)} %get-tuple-element.114.refs_1_, ...), custom_call_target="tpu_custom_call" | custom-call | tf_op jit(solution)/shard_map/mlp_backward/pallas_call | solution.py:311
  365.9 109.8 %attention_backward.2 = (bf16[1024,1024]{1,0:T(8,128)(2,1)}, bf16[1024,1024]{1,0:T(8,128)(2,1)}, bf16[1024,1024]{1,0:T(8,128)(2,1)}, bf16[1024,1024]{1,0:T(8,128...) custom-call(f32[640,1024]{1,0:T(8,128)} %get-tuple-element.119.refs_, ...), custom_call_target="tpu_custom_call" | custom-call | tf_op jit(solution)/shard_map/attention_backward/pallas_call | solution.py:311
  475.7 64.7 %mlp_backward.3 = (bf16[4096,1024]{1,0:T(8,128)(2,1)}, bf16[1024,4096]{1,0:T(8,128)(2,1)}, f32[640,1024]{1,0:T(8,128)}, bf16[640,1024]{1,0:T(8,128)(2,1)}, f32[1...) custom-call(f32[640,1024]{1,0:T(8,128)} %get-tuple-element.128.refs_, ...), custom_call_target="tpu_custom_call" | custom-call | tf_op jit(solution)/shard_map/mlp_backward/pallas_call | solution.py:311
  540.4 107.6 %attention_backward.3 = (bf16[1024,1024]{1,0:T(8,128)(2,1)}, bf16[1024,1024]{1,0:T(8,128)(2,1)}, bf16[1024,1024]{1,0:T(8,128)(2,1)}, bf16[1024,1024]{1,0:T(8,128...) custom-call(f32[640,1024]{1,0:T(8,128)} %get-tuple-element.138.refs_, ...), custom_call_target="tpu_custom_call" | custom-call | tf_op jit(solution)/shard_map/attention_backward/pallas_call | solution.py:311
  648.0 2.0 slice.110
  650.1 2.9 copy.54
  657.8 1.5 stack.46
  659.3 1.4 convert_reduce_fusion.1
  665.6 1.5 stack.45
  668.6 1.6 reshape.229
  671.7 56.7 %scatter.1 = (f32[32,1024]{1,0:T(8,128)}, f32[32,1024]{1,0:T(8,128)}, f32[32,1024]{1,0:T(8,128)}, f32[32,1024]{1,0:T(8,128)}, f32[16,256]{1,0:T(8,128)}) custom-call(bf16[2,2,4,2,32,1024]{5,4,3,2,1,0:T(8,128)(2,1)} %bitcast.113, bf16[2,2,4,2,32,1024]{5,4,3,2,1,0:T(8,128)(2,1)} %bitcast.114, bf16[2,2,4,2,32,1024]{5,4,3,2,1,0:T(8,128)(2,1)} %bitcast.115, ...), custom_call_target="tpu_custom_call" | custom-call | tf_op jit(solution)/shard_map/scatter/pallas_call | solution.py:311
  729.6 3.3 multiply_subtract_fusion.2
  734.0 2.2 multiply_subtract_fusion.1
  736.9 2.2 multiply_subtract_fusion
  (105 shorter events, 24.1 us)
Async XLA Ops:
  2.6 3.2 copy-start.24
  2.6 3.9 copy-start.2
  2.7 4.7 copy-start.8
  6.6 2.4 copy-start.1
  317.3 3.4 copy-start.3
  650.0 3.0 copy-start.17
  650.0 3.0 copy-start.18
  650.0 3.0 copy-start.19
  650.0 3.0 copy-start.26
  650.1 3.7 copy-start.22
  650.1 3.7 copy-start.23
  729.5 3.4 copy-start.13
  729.5 3.4 copy-start.14
  729.5 3.4 copy-start.15
  729.5 3.4 copy-start.16
  729.6 4.4 copy-start.4
  729.6 4.4 copy-start.5
  729.6 4.3 copy-start.10
  729.6 4.3 copy-start.12
  734.0 2.6 copy-start.9
  734.0 2.9 copy-start.11
  736.9 2.3 copy-start.25
  736.9 2.3 copy-start.28
  736.9 2.3 copy-start.29
  (6 other events, 10.1 us)

commit v3 on v2

v3 whole, which is shorter than its diff:
```python
import functools
import math

import jax
import jax.numpy as jnp
from jax import lax
from jax.experimental import pallas as pl
from jax.experimental.pallas import tpu as pltpu
from jax.sharding import PartitionSpec as P

STEP = 10
beta_first = 0.9
beta_second = 0.999
adam_eps = 1e-08
MESH = pl.DeviceIdType.MESH
ALL = slice(None)
D = 1024
HEADS = 16
HEAD_DIM = 64
FF = 4096
SEQ = 145
SPAN = 160
GROUP = 256
FF_TILE = 512
ROWS = 16
norm_eps = 1e-06
LOW = jnp.bfloat16
FULL = jnp.float32
GAIN_A, SHIFT_A, BIAS_Q, BIAS_V, BIAS_O, SCALE_A, GAIN_M, SHIFT_M, BIAS_D, SCALE_M, BIAS_U = range(11)


class Shape:
    def __init__(self, mesh):
        chips = mesh.shape["chip"]
        self.X = mesh.shape["node"] // 2
        self.Q = 2 ** ((chips.bit_length() - 1) // 2)
        self.P = chips // self.Q
        self.devices = mesh.shape["node"] * chips
        self.grid = (self.X, 2, self.P, self.Q)
        self.sizes = {"x": self.X, "c": 2, "p": self.P, "q": self.Q}


class Place:
    def __init__(self, shape):
        self.sizes = shape.sizes
        node, chip = lax.axis_index("node"), lax.axis_index("chip")
        self.at = {"x": node // 2, "c": lax.rem(node, 2), "p": chip // shape.Q, "q": lax.rem(chip, shape.Q)}
        self.offs, self.devices = {}, {}
        for axis, n in shape.sizes.items():
            for k in range(1, n):
                off = lax.rem(self.at[axis] + k, n)
                to = dict(self.at, **{axis: off})
                self.offs[axis, k] = off
                self.devices[axis, k] = (to["x"] * 2 + to["c"], to["p"] * shape.Q + to["q"])

    def off(self, axis, k):
        return self.offs[axis, k % self.sizes[axis]]

    def greet(self):
        barrier = pltpu.get_barrier_semaphore()
        for device in self.devices.values():
            pl.semaphore_signal(barrier, inc=1, device_id=device, device_id_type=MESH)
        pl.semaphore_wait(barrier, len(self.devices))


class Move:
    def __init__(self, src, dst, came, sems, device):
        if device is None:
            copy = functools.partial(pltpu.make_async_copy, src, dst, sems[0])
            self.start, self.arrived, self.sent = lambda: copy().start(), lambda: copy().wait(), None
        else:
            copy = functools.partial(
                pltpu.make_async_remote_copy,
                send_sem=sems[0], recv_sem=sems[1], device_id=device, device_id_type=MESH)
            self.start = lambda: copy(src, dst).start()
            self.sent = lambda: copy(src, dst).wait_send()
            self.arrived = lambda: copy(came, came).wait_recv()


class Task:
    def __init__(self, place, sems):
        self.place, self.sems, self.used = place, sems, 0
        self.phases = [([], [], []) for _ in range(5)]

    def move(self, begin, end, src, dst, came=None, axis=None, k=None):
        slot, self.used = self.used, self.used + 1
        sems = (self.sems[0].at[slot], self.sems[1].at[slot])
        move = Move(src, dst, dst if came is None else came, sems, None if axis is None else self.place.devices[axis, k])
        self.phases[begin][2].append(move)
        self.phases[end][0].append(move)


def plan(events):
    todo, flying = {}, []
    for time, task, phase in sorted(events, key=lambda e: (e[0], -e[2])):
        waits, work, starts = task.phases[phase]
        acts = todo.setdefault(time, [])
        acts += [move.arrived for move in waits] + work + [move.start for move in starts]
        acts += [move.sent for move in waits if move.sent is not None]
        flying = [move for move in flying if move not in waits] + starts
    return todo, [move.arrived for move in flying] + [move.sent for move in flying if move.sent is not None]


class Gather(Task):
    def __init__(self, place, src, dst, cols, order, sems):
        super().__init__(place, sems)
        at, sizes = place.at, place.sizes
        one, two, three = order

        def region(**fix):
            pick = dict(at, **fix)
            return dst.at[pick["x"], pick["c"], pick["p"], pick["q"], :, cols]

        def push(begin, end, axis, k, own=None, **held):
            came = region(**dict(held, **{axis: place.off(axis, -k)}))
            self.move(begin, end, region(**held) if own is None else own, region(**held), came, axis, k)

        own = src.at[:, cols]
        self.move(0, 1, own, region())
        for k in range(1, sizes[one]):
            push(0, 1, one, k, own)
        for k in range(1, sizes[two]):
            push(1, 2, two, k, **{one: ALL})
        push(1, 4, "c", 1, **{one: ALL})
        for k in range(1, sizes[three]):
            push(2, 3, three, k, **{one: ALL, two: ALL})
        for k in range(1, sizes[two]):
            push(2, 4, "c", 1, **{one: ALL, two: place.off(two, k)})
        for k in range(1, sizes[three]):
            push(3, 4, "c", 1, **{one: ALL, two: ALL, three: place.off(three, k)})


class Scatter(Task):
    def __init__(self, place, src, acc, out, order, bufs, sems, start, stop):
        super().__init__(place, sems)
        at, sizes = place.at, place.sizes
        self.start, self.stop = start, stop
        left = [a for a in "xpq" if a not in order[: max(start - 1, 0)]]

        def held(**fix):
            x, p, q = [fix.get(a, ALL) for a in "xpq"]
            return src.at[x, at["c"], p, q] if acc is None else acc.at[tuple(fix.get(a, ALL) for a in left)]

        def add(view, terms):
            if len(terms) == 1:
                view[...] = view[...] + terms[0][...]
            else:
                view[...] = sum([term[...].astype(FULL) for term in terms], view[...].astype(FULL)).astype(LOW)

        def finish():
            last = order[2]
            total = held(**at)[...].astype(FULL)
            for k in range(1, sizes[last]):
                total = total + bufs[3][k - 1].astype(FULL)
            out[...] = total

        if start > 0:
            self.move(start - 1, start, src, acc)
        else:
            if acc is not None:
                self.move(0, 1, src.at[:, at["c"]], acc)
            self.move(0, 1, src.at[:, place.off("c", 1)], bufs[0], None, "c", 1)
            for i in range(sizes["x"]):
                self.phases[1][1].append(functools.partial(add, held(x=i), [bufs[0].at[i]]))
        known = {}
        for phase, axis in enumerate(order, 1):
            if phase >= start:
                for k in range(1, sizes[axis]):
                    away = held(**dict(known, **{axis: place.off(axis, k)}))
                    if phase < stop:
                        self.move(phase, phase + 1, away, bufs[phase].at[k - 1], None, axis, k)
            known[axis] = at[axis]
            if start <= phase < min(3, stop):
                terms = [bufs[phase].at[k - 1] for k in range(1, sizes[axis])]
                self.phases[phase + 1][1].append(functools.partial(add, held(**known), terms))
        if stop > 4:
            self.phases[4][1].append(finish)
        self.left_over = held(**{a: at[a] for a in order[: max(stop - 1, 0)]})


class Spill(Task):
    def __init__(self, place, src, dst, sems):
        super().__init__(place, sems)
        self.move(0, 1, src, dst)


class Total(Task):
    def __init__(self, place, src, out, bufs, sems):
        super().__init__(place, sems)
        stages = [src] + list(bufs[4:]) + [out]

        def add(i):
            total = stages[i][...]
            for k in range(1, place.sizes["cxqp"[i]]):
                total = total + bufs[i][k - 1]
            stages[i + 1][...] = total

        for i, axis in enumerate("cxqp"):
            for k in range(1, place.sizes[axis]):
                self.move(i, i + 1, stages[i], bufs[i].at[k - 1], None, axis, k)
            self.phases[i + 1][1].append(functools.partial(add, i))


ANYWHERE = pl.BlockSpec(memory_space=pl.ANY)


ORDERS = (("x", "q", "p"), ("q", "x", "p")) * 2 + (("x", "p", "q"), ("q", "p", "x"))


class Piece:
    def __init__(self, block, source, order):
        self.block, self.source, self.order, self.done, self.sum = block, source, ORDERS[order % len(ORDERS)], 0, None


class Scattering:
    def __init__(self, shape, ticks, entries, spills=(), total=None, last=False):
        self.shape, self.ticks, self.spills, self.total = shape, ticks, spills, total
        self.aliases, self.scratch, self.inputs, self.made = {}, [], [], []
        self.out_shape, self.out_specs = [], []
        sizes = shape.sizes
        blocks = {}
        for piece, tick, lag in entries:
            first = piece.done
            times = {f: tick + lag * f for f in range(5)} if first == 0 else {
                f: tick if f < first else tick + 1 + lag * (f - first) for f in range(first - 1, 5)}
            stop = 5 if last else min([f for f, time in times.items() if time >= ticks] + [5])
            stop = 5 if stop == 4 else stop
            buffers, index = {}, {}
            if piece.source[0] != "own":
                axes = [sizes[a] for a in "xpq" if a not in piece.order[: max(first - 1, 0)]]
                buffers["acc"] = tuple(axes) + piece.block
            if first == 0:
                buffers[0] = tuple(sizes[a] for a in "xpq") + piece.block
            for f, axis in enumerate(piece.order, 1):
                if first <= f < stop:
                    rest = [sizes[a] for a in "xpq" if a not in piece.order[:f]]
                    buffers[f] = (sizes[axis] - 1, *rest) + piece.block
            for key, buffer in buffers.items():
                index[key] = len(self.scratch)
                self.scratch.append(pltpu.VMEM(buffer, LOW))
            if piece.source[0] != "own" and not any(piece.source[1] is a for a in self.inputs):
                self.inputs.append(piece.source[1])
            if stop == 5:
                blocks.setdefault(piece.block, []).append(piece)
            self.made.append([piece, times, stop, index])
        for block, pieces in blocks.items():
            for i, piece in enumerate(pieces):
                piece.target = (len(self.out_shape), i)
            self.out_shape.append(jax.ShapeDtypeStruct((len(pieces),) + block, FULL))
            self.out_specs.append(whole(self.out_shape[-1].shape))
        for piece, _, stop, _ in self.made:
            if stop < 5:
                piece.target = (len(self.out_shape), None)
                axes = [sizes[a] for a in "xpq" if a not in piece.order[: stop - 1]]
                self.out_shape.append(jax.ShapeDtypeStruct(tuple(axes) + piece.block, LOW))
                self.out_specs.append(ANYWHERE)
        self.first_spill = len(self.out_shape)
        for _, _, _, block in spills:
            self.out_shape.append(jax.ShapeDtypeStruct(block, LOW))
            self.out_specs.append(ANYWHERE)
        if total is not None:
            self.first_total = len(self.scratch)
            self.scratch += [pltpu.VMEM((sizes[a] - 1,) + total[1], FULL) for a in "cxqp"]
            self.scratch += [pltpu.VMEM(total[1], FULL)] * 3
            self.out_shape.append(jax.ShapeDtypeStruct(total[1], FULL))
            self.out_specs.append(whole(total[1]))
        self.in_specs = [ANYWHERE] * len(self.inputs)
        copies = max(3 + sum(sizes[a] - 1 for a in "xpq"), sum(n - 1 for n in sizes.values()))
        self.scratch += [pltpu.SemaphoreType.DMA((len(self.made) + len(spills) + 1, copies))] * 2

    def build(self, ins, outs, scratch, own):
        place = Place(self.shape)
        send, recv = scratch[-2:]
        events, halted, slot = [], [], 0
        for piece, times, stop, index in self.made:
            kind, base, lead = piece.source
            if kind == "own":
                src = own[base].at[lead]
            else:
                src = ins[[a is base for a in self.inputs].index(True)]
                src = src if lead is None else src.at[lead]
            bufs = {key: scratch[i] for key, i in index.items()}
            o, i = piece.target
            out = outs[o].at[i] if stop == 5 else outs[o]
            task = Scatter(
                place, src, bufs.get("acc"), out, piece.order, bufs, (send.at[slot], recv.at[slot]), piece.done, stop)
            slot += 1
            events += [(time, task, f) for f, time in times.items() if f < stop]
            if stop < 5:
                halted.append((task, out))
        for n, (tick, base, lead, _) in enumerate(self.spills):
            task = Spill(place, own[base].at[lead], outs[self.first_spill + n], (send.at[slot], recv.at[slot]))
            slot += 1
            events.append((tick, task, 0))
        if self.total is not None:
            task = Total(
                place, own[self.total[0]], outs[-1], scratch[self.first_total : -2], (send.at[slot], recv.at[slot]))
            events += [(self.ticks + 2 * f, task, f) for f in range(5)]
        todo, rest = plan(events)
        moves = []
        for task, out in halted:
            rest += task.phases[task.stop][1]
            move = Move(task.left_over, out, None, (task.sems[0].at[task.used],), None)
            rest.append(move.start)
            moves.append(move.arrived)
        return place, todo, rest + moves

    def take(self, outs):
        for piece, _, stop, _ in self.made:
            o, i = piece.target
            if stop == 5:
                piece.sum = (outs[o], i)
            else:
                piece.source, piece.done = ("part", outs[o], None), stop
        self.spilled = outs[self.first_spill : self.first_spill + len(self.spills)]
        self.result = outs[-1]


def beside(kernel, points, transfer, number, grid, inputs, in_specs, out_specs, out_shape, scratch, name, limit=62):
    total = grid * points
    counts = [len(inputs), len(transfer.inputs) if transfer else 0, len(out_shape), len(transfer.out_shape) if transfer else 0, len(scratch)]

    def body(*refs):
        groups, i = [], 0
        for n in counts:
            groups.append(refs[i : i + n])
            i += n
        groups.append(refs[i:])
        step = pl.program_id(0)
        if transfer is None:
            kernel(lambda point: None, *groups[0], *groups[2], *groups[4])
            return
        place, todo, rest = transfer.build(groups[1], groups[3], groups[5], groups[4])

        def tick(point):
            if point == 0:
                pl.when(step == 0)(place.greet)
            for time in sorted(todo):
                if time < total and time % points == point:
                    @pl.when(step == time // points)
                    def _():
                        for act in todo[time]:
                            act()

        kernel(tick, *groups[0], *groups[2], *groups[4])

        @pl.when(step == grid - 1)
        def _():
            for act in [act for time in sorted(todo) if time >= total for act in todo[time]] + rest:
                act()

    extra = {}
    if transfer is not None:
        extra["input_output_aliases"] = {counts[0] + i: counts[2] + o for i, o in transfer.aliases.items()}
        inputs, in_specs = list(inputs) + transfer.inputs, list(in_specs) + transfer.in_specs
        out_specs, out_shape = list(out_specs) + transfer.out_specs, list(out_shape) + transfer.out_shape
        scratch = list(scratch) + transfer.scratch
    outs = pl.pallas_call(
        body,
        grid=(grid,),
        in_specs=in_specs,
        out_specs=out_specs,
        out_shape=out_shape,
        scratch_shapes=scratch,
        name=name,
        compiler_params=pltpu.CompilerParams(
            dimension_semantics=("arbitrary",),
            vmem_limit_bytes=limit * 2**20,
            collective_id=None if transfer is None else number,
            has_side_effects=transfer is not None,
        ),
        **extra,
    )(*inputs)
    if transfer is not None:
        transfer.take(outs[counts[2] :])
    return outs[: counts[2]]


def mul(a, b):
    return jnp.dot(a, b, preferred_element_type=FULL)


def mul_nt(a, b):
    return lax.dot_general(a, b, (((1,), (1,)), ((), ())), preferred_element_type=FULL)


def mul_tn(a, b):
    return lax.dot_general(a, b, (((0,), (0,)), ((), ())), preferred_element_type=FULL)


def normalise(values):
    centred = values - jnp.mean(values, axis=-1, keepdims=True)
    inverse = lax.rsqrt(jnp.mean(centred * centred, axis=-1, keepdims=True) + norm_eps)
    return centred * inverse, inverse


def tiles(rows, step=160):
    return [slice(i, i + step) for i in range(0, rows, step)]


def row(vec, index):
    return vec[index : index + 1, :]


def softmax_of(q, k, lanes, width):
    scores = mul_nt(jnp.where(lanes, q, jnp.zeros_like(q)), k) * HEAD_DIM ** (-0.5)
    scores = jnp.where(width, scores, -1e30)
    expo = jnp.exp(scores - jnp.max(scores, axis=-1, keepdims=True))
    return expo * (1.0 / jnp.sum(expo, axis=-1, keepdims=True))


def lane_sets():
    lane = lax.broadcasted_iota(jnp.int32, (SPAN, 128), 1)
    return [lane < HEAD_DIM, lane >= HEAD_DIM]


def key_set():
    return lax.broadcasted_iota(jnp.int32, (SPAN, SPAN), 1) < SEQ


def whole(shape):
    return pl.BlockSpec(shape, lambda j: (0,) * len(shape), pipeline_mode=pl.Buffered(1))


def whole_of(layer, rows):
    return pl.BlockSpec((None, rows, D), lambda j: (layer, 0, 0), pipeline_mode=pl.Buffered(1))


def columns_of(layer, rows, width):
    return pl.BlockSpec((None, rows, width), lambda j: (layer, 0, j))


def columns(rows, width, at=0):
    return pl.BlockSpec((rows, width), lambda j: (0, j + at))


def lines(height, cols):
    return pl.BlockSpec((height, cols), lambda j: (j, 0))


def phi_of(u):
    return 0.5 * (1.0 + lax.erf(u * 0.5**0.5))


N_IN, N_UP, N_DOWN = D // GROUP, FF // FF_TILE, D // GROUP
ITEMS = N_IN + 1 + N_UP + N_DOWN
GATHER_LAG = 3
AHEAD = 4 * GATHER_LAG + 1
GATHER_ORDERS = (("p", "q", "x"), ("p", "x", "q")) * 2 + (("q", "p", "x"), ("x", "p", "q"))


def item_of(number):
    if number < N_IN:
        return 0, number, pl.ds(number * 3 * GROUP, 3 * GROUP)
    number -= N_IN
    if number == 0:
        return 1, 0, pl.ds(0, D)
    number -= 1
    if number < N_UP:
        return 2, number, pl.ds(number * FF_TILE, FF_TILE)
    return 3, number - N_UP, pl.ds((number - N_UP) * GROUP, GROUP)


def matrix_of(ref):
    value = ref[...]
    flat = (-1, value.shape[-1])
    return value.reshape(flat) if value.shape[-2] % 16 == 0 else value.astype(FULL).reshape(flat).astype(LOW)


def forward_kernel(shape, layers, *refs):
    count = 4 * layers
    tokens, packed, *sources = refs[: 2 + count]
    refs = refs[2 + count :]
    a_out, q_out, k_out, v_out, mixed_out, branch_out, mid_out, c_out, u_out, act_out, down_out, vec_out, next_out, low_out = refs[:14]
    gathered, refs = refs[14 : 14 + count], refs[14 + count :]
    h, act, vec = refs[:3]
    slots, sums, (send, recv, loaded) = refs[3:7], refs[7:14], refs[14:]
    step = pl.program_id(0)
    rows = h.shape[0]
    place = Place(shape)
    total = layers * ITEMS
    jobs, loads, n = [], [], 1
    for layer in range(layers):
        for number in range(ITEMS):
            weight, index, cols = item_of(number)
            src, dst = sources[4 * layer + weight], gathered[4 * layer + weight]
            half, job = cols.size // 2, []
            for i in range(2):
                part = pl.ds(cols.start + i * half, half)
                order = GATHER_ORDERS[(n - 1) % len(GATHER_ORDERS)]
                job.append(Gather(place, src, dst, part, order, (send.at[n], recv.at[n])))
                n += 1
            jobs.append(job)
            slot = index % slots[weight].shape[0]
            loads.append(
                functools.partial(
                    pltpu.make_async_copy, dst.at[:, :, :, :, :, cols], slots[weight].at[slot], loaded.at[weight, slot]))
    jobs[0].append(Total(place, packed, vec_out, sums, (send.at[0], recv.at[0])))
    todo, _ = plan([
        (i + GATHER_LAG * phase, task, phase) for i, job in enumerate(jobs) for task in job for phase in range(5)])

    pl.when(step == 0)(place.greet)
    for s in range(total + AHEAD):
        @pl.when(step == s)
        def _():
            if 0 <= s - AHEAD < total:
                loads[s - AHEAD]().wait()
            for act in todo.get(s, []):
                act()
            if 0 <= s - AHEAD + 1 < total:
                loads[s - AHEAD + 1]().start()

    at = step - AHEAD
    item = jnp.maximum(lax.rem(jnp.maximum(at, 0), ITEMS), 0)
    layer = jnp.maximum(at, 0) // ITEMS
    live = at >= 0
    base = pl.multiple_of(layer * ROWS, ROWS)

    def line(index):
        return vec[pl.ds(index, 1), :]

    @pl.when(at == 0)
    def _():
        h[...] = tokens[...]

    @pl.when(live & (item == 0))
    def _():
        vec[...] = vec_out[pl.ds(base, ROWS), :]
        for t in tiles(rows):
            normal, _ = normalise(h[t, :])
            a_out[0, t, :] = (normal * line(GAIN_A) + line(SHIFT_A)).astype(LOW)

    @pl.when(live & (item < N_IN))
    def _():
        group = pl.ds(pl.multiple_of(item * GROUP, GROUP), GROUP)
        proj = mul(a_out[0], matrix_of(slots[0].at[lax.rem(item, 2)]))
        q_out[0] = (proj[:, :GROUP] + vec[BIAS_Q : BIAS_Q + 1, group]).astype(LOW)
        k_out[0] = proj[:, GROUP : 2 * GROUP].astype(LOW)
        v_out[0] = (proj[:, 2 * GROUP :] + vec[BIAS_V : BIAS_V + 1, group]).astype(LOW)
        lanes, width = lane_sets(), key_set()

        def image(i, carry):
            t = pl.ds(pl.multiple_of(i * SPAN, SPAN), SPAN)
            done = []
            for pair in range(GROUP // 128):
                cols = slice(pair * 128, pair * 128 + 128)
                q, k, v = q_out[0, t, cols], k_out[0, t, cols], v_out[0, t, cols]
                both = [mul(softmax_of(q, k, lanes[s], width).astype(LOW), v) for s in range(2)]
                done.append(jnp.where(lanes[0], both[0], both[1]).astype(LOW))
            mixed_out[0, t, group] = jnp.concatenate(done, axis=1)
            return carry

        lax.fori_loop(0, rows // SPAN, image, 0)

    @pl.when(live & (item == N_IN))
    def _():
        weight = matrix_of(slots[1].at[0])
        for t in tiles(rows):
            branch = mul(mixed_out[0, t, :], weight) + line(BIAS_O)
            branch_out[0, t, :] = branch
            middle = h[t, :] + line(SCALE_A) * branch
            mid_out[0, t, :] = middle
            normal, _ = normalise(middle)
            c_out[0, t, :] = (normal * line(GAIN_M) + line(SHIFT_M)).astype(LOW)

    @pl.when(live & (item > N_IN) & (item <= N_IN + N_UP))
    def _():
        tile = item - N_IN - 1
        per = D // FF_TILE
        bias = vec[pl.ds(BIAS_U + tile // per, 1), pl.ds(pl.multiple_of(lax.rem(tile, per) * FF_TILE, FF_TILE), FF_TILE)]
        u = mul(c_out[0], matrix_of(slots[2].at[lax.rem(tile, 2)])) + bias
        u_out[0] = u
        active = (u * phi_of(u)).astype(LOW)
        act_out[0] = active
        act[:, pl.ds(pl.multiple_of(tile * FF_TILE, FF_TILE), FF_TILE)] = active

    @pl.when(live & (item > N_IN + N_UP))
    def _():
        tile = item - N_IN - 1 - N_UP
        group = pl.ds(pl.multiple_of(tile * GROUP, GROUP), GROUP)
        down = mul(act[...], matrix_of(slots[3].at[lax.rem(tile, 2)])) + vec[BIAS_D : BIAS_D + 1, group]
        down_out[0, :, group] = down
        h[:, group] = mid_out[0, :, group] + vec[SCALE_M : SCALE_M + 1, group] * down

    @pl.when(at == ITEMS - 1)
    def _():
        next_out[...] = h[...]

    @pl.when(at == total - 1)
    def _():
        low_out[...] = h[...].astype(LOW)


def forward(shape, layers, tokens, packed, sources, number):
    rows = tokens.shape[0]
    total = layers * ITEMS

    def spot(s):
        at = jnp.clip(s - AHEAD, 0, total - 1)
        return at // ITEMS, lax.rem(at, ITEMS)

    def out(width, dtype, pick=None, block=D):
        def index(s):
            layer, item = spot(s)
            return layer, 0, 0 if pick is None else pick(item)

        return jax.ShapeDtypeStruct((layers, rows, width), dtype), pl.BlockSpec((1, rows, block), index)

    def one(spec_shape, dtype):
        return jax.ShapeDtypeStruct(spec_shape, dtype), whole(spec_shape)

    group = lambda item: jnp.minimum(item, N_IN - 1)
    tile = lambda item: jnp.clip(item - N_IN - 1, 0, N_UP - 1)
    qkv = [out(D, LOW, group, GROUP)] * 3
    outs = [out(D, LOW)] + qkv + [out(D, LOW), out(D, FULL), out(D, FULL), out(D, LOW)]
    outs += [out(FF, FULL, tile, FF_TILE), out(FF, LOW, tile, FF_TILE), out(D, FULL)]
    outs += [one(packed.shape, FULL), one((rows, D), FULL), one((rows, D), LOW)]
    outs += [(jax.ShapeDtypeStruct(shape.grid + b.shape, LOW), ANYWHERE) for b in sources]
    sizes = shape.sizes
    tasks = 2 * total + 1
    copies = 1 + sum(sizes[a] - 1 for a in "xpq") + 1 + 2 * (max(sizes.values()) - 1)
    deep = [b.shape[0] for b in sources[:4]]
    slots = [
        pltpu.VMEM((count,) + shape.grid + (depth, width), LOW)
        for count, depth, width in zip((2, 1, 2, 2), deep, (3 * GROUP, D, FF_TILE, GROUP))
    ]
    return pl.pallas_call(
        functools.partial(forward_kernel, shape, layers),
        grid=(total + AHEAD,),
        in_specs=[whole((rows, D)), whole(packed.shape)] + [ANYWHERE] * len(sources),
        out_specs=[o[1] for o in outs],
        out_shape=[o[0] for o in outs],
        scratch_shapes=[pltpu.VMEM((rows, D), FULL), pltpu.VMEM((rows, FF), LOW), pltpu.VMEM((ROWS, D), FULL)]
        + slots
        + [pltpu.VMEM((sizes[a] - 1,) + packed.shape, FULL) for a in "cxqp"]
        + [pltpu.VMEM(packed.shape, FULL)] * 3
        + [pltpu.SemaphoreType.DMA((tasks, copies))] * 2
        + [pltpu.SemaphoreType.DMA((4, 2))],
        name="forward",
        compiler_params=pltpu.CompilerParams(
            dimension_semantics=("arbitrary",), vmem_limit_bytes=60 * 2**20, collective_id=number, has_side_effects=True),
    )(tokens, packed, *sources)


def norm_back(values, upstream, gain):
    normal, inverse = normalise(values)
    scaled = upstream * gain
    inner = (
        scaled
        - jnp.mean(scaled, axis=-1, keepdims=True)
        - normal * jnp.mean(scaled * normal, axis=-1, keepdims=True)
    )
    return inverse * inner, upstream * normal


def summed(values):
    return jnp.sum(values, axis=0, keepdims=True)


def mlp_bwd(tick, g, down, mid, branch, c, vec, u, act, wu, wd, g_down, d_mid, db_out, sums, d_bias_u, dd, stage):
    step, last = pl.program_id(0), pl.num_programs(0) - 1
    rows = g.shape[0]
    tick(0)

    @pl.when(step == 0)
    def _():
        sums[...] = jnp.zeros_like(sums)
        for t in tiles(rows):
            grad = g[t, :]
            scaled = grad * row(vec, SCALE_M)
            sums[SCALE_M : SCALE_M + 1, :] += summed(grad * down[t, :])
            sums[BIAS_D : BIAS_D + 1, :] += summed(scaled)
            dd[t, :] = scaled.astype(LOW)
        d_mid[...] = jnp.zeros_like(d_mid)

    d_act = mul_nt(dd[...], wd[...])
    upper = u[...]
    density = jnp.exp(-0.5 * upper * upper) * (2.0 * math.pi) ** (-0.5)
    du = d_act * (phi_of(upper) + upper * density)
    d_bias_u[...] = summed(du)
    du_b = du.astype(LOW)
    stage[step] = mul_tn(c[...], du_b).reshape(stage.shape[1:]).astype(LOW)
    tick(1)
    g_down[...] = mul_tn(act[...], dd[...]).astype(LOW)
    d_mid[...] += mul_nt(du_b, wu[...])

    @pl.when(step == last)
    def _():
        for t in tiles(rows):
            upstream = d_mid[t, :]
            through, gain_terms = norm_back(mid[t, :], upstream, row(vec, GAIN_M))
            sums[GAIN_M : GAIN_M + 1, :] += summed(gain_terms)
            sums[SHIFT_M : SHIFT_M + 1, :] += summed(upstream)
            middle = g[t, :] + through
            d_mid[t, :] = middle
            sums[SCALE_A : SCALE_A + 1, :] += summed(middle * branch[t, :])
            db = middle * row(vec, SCALE_A)
            sums[BIAS_O : BIAS_O + 1, :] += summed(db)
            db_out[t, :] = db.astype(LOW)


def mlp_backward(layer, g, down, mid, branch, c, vec, u, act, w_up, w_down, shape, transfer, number):
    rows = g.shape[0]
    f32, low = lambda s: jax.ShapeDtypeStruct(s, FULL), lambda s: jax.ShapeDtypeStruct(s, LOW)
    full = whole((rows, D))
    tile = columns_of(layer, rows, FF_TILE)
    steps = FF // FF_TILE
    return beside(
        mlp_bwd,
        points=MLP_POINTS,
        transfer=transfer,
        number=number,
        grid=steps,
        inputs=[g, down, mid, branch, c, vec, u, act, w_up, w_down],
        in_specs=[full] + [whole_of(layer, rows)] * 4
        + [whole(vec.shape), tile, tile, columns(D, FF_TILE), lines(FF_TILE, D)],
        out_specs=[lines(FF_TILE, D), full, full, whole((ROWS, D)), columns(1, FF_TILE)],
        out_shape=[low((FF, D)), f32((rows, D)), low((rows, D)), f32((ROWS, D)), f32((1, FF))],
        scratch=[
            pltpu.VMEM((rows, D), LOW),
            pltpu.VMEM((steps,) + shape.grid + (D // shape.devices, FF_TILE), LOW),
        ],
        name="mlp_backward",
    )


def attend_bwd(tick, d_mid, db, h, a, vec, mixed, rest, q, k, v, wq, wk, wv, wo, g_out, sums, dq, dk, dv, dm, stage, values):
    step, last = pl.program_id(0), pl.num_programs(0) - 1
    rows = h.shape[0]
    tick(0)

    @pl.when(step == 0)
    def _():
        sums[...] = jnp.zeros_like(sums)
        g_out[...] = jnp.zeros_like(g_out)

    def store(kind, term):
        stage[step, kind] = term.reshape(stage.shape[2:]).astype(LOW)

    group = pl.ds(pl.multiple_of(step * GROUP, GROUP), GROUP)
    dm[...] = mul_nt(db[...], wo[...]).astype(LOW)
    store(3, mul_tn(mixed[...], db[:, group]))
    lanes, width = lane_sets(), key_set()

    def image(i, carry):
        at = pl.ds(pl.multiple_of(i * SPAN, SPAN), SPAN)
        bias = []
        for pair in range(GROUP // 128):
            cols = slice(pair * 128, pair * 128 + 128)
            qp, kp, vp, dmp = q[at, cols], k[at, cols], v[at, cols], dm[at, cols]
            grads = []
            for s in range(2):
                prob = softmax_of(qp, kp, lanes[s], width)
                d_prob = mul_nt(jnp.where(lanes[s], dmp, jnp.zeros_like(dmp)), vp)
                ds = (prob * (d_prob - jnp.sum(prob * d_prob, axis=-1, keepdims=True))).astype(LOW)
                grads.append((mul(ds, kp), mul_tn(ds, qp), mul_tn(prob.astype(LOW), dmp)))
            d_q, d_k, d_v = [jnp.where(lanes[0], one, two) for one, two in zip(*grads)]
            d_q, d_k = d_q * HEAD_DIM ** (-0.5), d_k * HEAD_DIM ** (-0.5)
            dq[at, cols], dk[at, cols], dv[at, cols] = d_q.astype(LOW), d_k.astype(LOW), d_v.astype(LOW)
            bias.append((summed(d_q), summed(d_v)))
        sums[BIAS_Q : BIAS_Q + 1, group] += jnp.concatenate([b[0] for b in bias], axis=1)
        sums[BIAS_V : BIAS_V + 1, group] += jnp.concatenate([b[1] for b in bias], axis=1)
        return carry

    images = rows // SPAN
    lax.fori_loop(0, images // 2, image, 0)
    tick(1)
    lax.fori_loop(images // 2, images, image, 0)
    for kind, term in enumerate((dq, dk, dv)):
        store(kind, mul_tn(a[...], term[...]))
    tick(2)
    g_out[...] += mul_nt(dq[...], wq[...]) + mul_nt(dk[...], wk[...]) + mul_nt(dv[...], wv[...])

    @pl.when(step == last)
    def _():
        for t in tiles(rows):
            upstream = g_out[t, :]
            through, gain_terms = norm_back(h[t, :], upstream, row(vec, GAIN_A))
            sums[GAIN_A : GAIN_A + 1, :] += summed(gain_terms)
            sums[SHIFT_A : SHIFT_A + 1, :] += summed(upstream)
            g_out[t, :] = d_mid[t, :] + through
        values[...] = rest[...]
        values[:ROWS, :] += sums[...]


def attention_backward(layer, d_mid, db, h, a, vec, mixed, rest, q, k, v, w_in, w_out, shape, transfer, number):
    rows = h.shape[0]
    n = D // GROUP
    f32 = lambda s: jax.ShapeDtypeStruct(s, FULL)
    full = whole((rows, D))
    cols = columns_of(layer, rows, GROUP)
    return beside(
        attend_bwd,
        points=ATTEND_POINTS,
        transfer=transfer,
        number=number,
        grid=n,
        inputs=[d_mid, db, h, a, vec, mixed, rest, q, k, v, w_in, w_in, w_in, w_out],
        in_specs=[full] * 3
        + [whole_of(layer, rows), whole(vec.shape), whole_of(layer, rows), whole(rest.shape)]
        + [cols] * 3
        + [pl.BlockSpec((D, GROUP), lambda j, m=m: (0, 3 * j + m)) for m in range(3)]
        + [lines(GROUP, D)],
        out_specs=[full, whole((ROWS, D))],
        out_shape=[f32((rows, D)), f32((ROWS, D))],
        scratch=[pltpu.VMEM((rows, GROUP), LOW)] * 4
        + [
            pltpu.VMEM((n, 4) + shape.grid + (D // shape.devices, GROUP), LOW),
            pltpu.VMEM(rest.shape, FULL),
        ],
        name="attention_backward",
    )


MLP_POINTS, MLP_LAG = 2, 3
ATTEND_POINTS = 3
TOP_LAG = 2
END_LAG = 2
MLP_TICKS, ATTEND_TICKS = MLP_POINTS * N_UP, ATTEND_POINTS * N_IN
TOP_UP = (1, 3, 5, 7, 9, 11, 13, 15)
TOP_DOWN = (1, 2, 5, 6, 9, 10, 11, 11)
TOP_IN = (3, 4, 7, 8)
LOW_LEFT = (2, 3, 5, 6)
LOW_UP = (7, 9, 11, 13, 14, 15)
END_LEFT = (1, 2)
END_DOWN = (2, 3, 5, 6, 8, 9, 10, 10)
END_IN = (4, 4, 7, 7, 9, 9, 11, 11)


def resumed(pieces, lag):
    under_way = [piece for piece in pieces if piece.sum is None]
    return [(piece, i // 8, lag) for i, piece in enumerate(under_way)]


def shape_blocks(shape, term):
    return term.reshape(shape.grid + (term.shape[0] // shape.devices, term.shape[1]))


def spread_rows(tokens):
    return jnp.pad(tokens, ((0, 0), (0, SPAN - SEQ), (0, 0))).reshape(-1, D)


def adamw(weight, gradient, first, second, rate, decay):
    first_new = beta_first * first + (1.0 - beta_first) * gradient
    second_new = beta_second * second + (1.0 - beta_second) * gradient * gradient
    fix_first = 1.0 - beta_first**STEP
    fix_second = 1.0 - beta_second**STEP
    stepped = first_new / fix_first / (jnp.sqrt(second_new / fix_second) + adam_eps)
    return (weight - rate * (stepped + decay * weight), first_new, second_new)


def on_device(
    shape,
    tokens,
    cotangent,
    w_attn_in,
    w_attn_out,
    w_mlp_in,
    w_mlp_out,
    vectors,
    first_attn_in,
    first_attn_out,
    first_mlp_in,
    first_mlp_out,
    first_vectors,
    second_attn_in,
    second_attn_out,
    second_mlp_in,
    second_mlp_out,
    second_vectors,
):
    shards = (w_attn_in, w_attn_out, w_mlp_in, w_mlp_out, vectors)
    layers, images = w_attn_in.shape[0], tokens.shape[0]
    mine = lax.axis_index(("node", "chip")) * vectors.shape[1]
    entries = D * (BIAS_U + FF // D)
    packed = lax.dynamic_update_slice_in_dim(
        jnp.zeros((layers, entries), FULL), lax.reduce_precision(vectors, 8, 7), mine, axis=1)
    packed = jnp.pad(packed, ((0, 0), (0, D * ROWS - entries))).reshape(layers * ROWS, D)
    sources = []
    for layer in range(layers):
        by_group = shards[0][layer].reshape(-1, 3, D // GROUP, GROUP).transpose(0, 2, 1, 3).reshape(-1, 3 * D)
        sources += [m.astype(LOW) for m in (by_group, w_attn_out[layer], w_mlp_in[layer], w_mlp_out[layer])]
    first = spread_rows(tokens.astype(FULL))
    outs = forward(shape, layers, first, packed, sources, 1)
    vec_rows, second, low = outs[11:14]
    weights = [w.reshape(-1, w.shape[-1]) for w in outs[14:]]
    kept = []
    for layer in range(layers):
        a, q, k, v, mixed, branch, mid, c, u, act, down = outs[:11]
        vec = vec_rows[layer * ROWS : layer * ROWS + ROWS]
        hidden = second if layer else first
        kept.append((vec, *weights[4 * layer : 4 * layer + 4], hidden, a, q, k, v, mixed, branch, mid, c, u, act, down))
    output = low.reshape(images, SPAN, D)[:, :SEQ]
    grad = spread_rows(cotangent.astype(FULL))
    high, deep = D // shape.devices, FF // shape.devices
    pieces, rest, left, number, order = [], jnp.zeros((0, D), FULL), [], 10, 0
    everything = [[[None] * (2 * N_UP), [None] * N_DOWN * 2, [None] * 4 * N_IN] for _ in range(layers)]

    def piece(layer, matrix, index, block, source):
        made = everything[layer][matrix][index] = Piece(block, source, index)
        pieces.append(made)
        return made

    for layer in reversed(range(layers)):
        vec, w_in, w_out, w_up, w_down, hidden, a, q, k, v, mixed, branch, mid, c, u, act, down = kept[layer]
        top = layer == layers - 1
        entries = resumed(pieces, MLP_LAG)
        for i, one in enumerate(left):
            entries.append((one, LOW_LEFT[i // 2], MLP_LAG))
        starts = TOP_UP if top else LOW_UP
        half = FF_TILE // 2
        for tile, start in enumerate(starts):
            for i in range(2):
                source = ("own", 1, (tile, ALL, ALL, ALL, ALL, ALL, pl.ds(i * half, half)))
                entries.append((piece(layer, 0, 2 * tile + i, (high, half), source), start, MLP_LAG))
        spills = [
            (MLP_TICKS, 1, tile, shape.grid + (high, FF_TILE)) for tile in range(len(starts), N_UP)]
        transfer = Scattering(shape, MLP_TICKS, entries, spills)
        g_down, d_mid, db, sums_m, d_bias_u = mlp_backward(
            layer, grad, down, mid, branch, c, vec, u, act, w_up, w_down, shape, transfer, number)
        lag = TOP_LAG if layer else END_LAG
        entries = resumed(pieces, lag)
        for n, tile in enumerate(range(len(starts), N_UP)):
            for i in range(2):
                source = ("hbm", transfer.spilled[n], (ALL, ALL, ALL, ALL, ALL, pl.ds(i * half, half)))
                entries.append((piece(layer, 0, 2 * tile + i, (high, half), source), END_LEFT[n], lag))
        spare = jnp.zeros((ROWS - BIAS_U - FF // D, D), FULL)
        rest = jnp.concatenate([sums_m[:BIAS_U], d_bias_u.reshape(-1, D), spare, rest])
        rest = jnp.pad(rest, ((0, 2 * ROWS - rest.shape[0]), (0, 0)))
        terms = shape_blocks(shape, g_down)
        for n, start in enumerate(END_DOWN if layer == 0 else TOP_DOWN):
            width = D // (2 * N_DOWN)
            source = ("hbm", terms, (ALL, ALL, ALL, ALL, ALL, pl.ds(n * width, width)))
            entries.append((piece(layer, 1, n, (deep, width), source), start, lag))
        starts = END_IN if layer == 0 else TOP_IN
        for n, start in enumerate(starts):
            for m in (2 * (n % 2), 2 * (n % 2) + 1):
                entries.append((piece(layer, 2, n // 2 * 4 + m, (high, GROUP), ("own", 4, (n // 2, m))), start, lag))
        spills = [
            (ATTEND_POINTS * tile + 2, 4, tile, (4,) + shape.grid + (high, GROUP)) for tile in range(len(starts) // 2, N_IN)]
        total = (5, (2 * ROWS, D)) if layer == 0 else None
        transfer = Scattering(shape, ATTEND_TICKS, entries, spills, total, layer == 0)
        grad, sums_a = attention_backward(
            layer, d_mid, db, hidden, a, vec, mixed, rest, q, k, v, w_in, w_out, shape, transfer, number + 1)
        left = [
            piece(layer, 2, tile * 4 + m, (high, GROUP), ("hbm", transfer.spilled[n], m))
            for n, tile in enumerate(range(len(starts) // 2, N_IN)) for m in range(4)]
        pieces = [one for one in pieces if one not in left]
        number += 2
        rest = rest[:ROWS] + sums_a
    totals = transfer.result.reshape(layers, ROWS, D)[:, : BIAS_U + FF // D].reshape(layers, -1)

    def joined(layer, matrix, pick=lambda i: True):
        found = [one.sum for i, one in enumerate(everything[layer][matrix]) if pick(i)]
        return jnp.concatenate([array[i] for array, i in found], axis=1)

    def joined_in(layer):
        return jnp.concatenate([joined(layer, 2, lambda i, m=m: i % 4 == m) for m in range(3)], axis=1)

    stacked = [
        jnp.stack([joined_in(layer) for layer in range(layers)]),
        jnp.stack([joined(layer, 2, lambda i: i % 4 == 3) for layer in range(layers)]),
        jnp.stack([joined(layer, 0) for layer in range(layers)]),
        jnp.stack([joined(layer, 1) for layer in range(layers)]),
        lax.dynamic_slice_in_dim(totals, mine, vectors.shape[1], axis=1),
    ]
    firsts = (first_attn_in, first_attn_out, first_mlp_in, first_mlp_out, first_vectors)
    seconds = (second_attn_in, second_attn_out, second_mlp_in, second_mlp_out, second_vectors)
    settings = (
        (D ** (-0.5), 0.05),
        ((D // 8) ** (-0.5), 0.05),
        (D ** (-0.5), 0.05),
        (FF ** (-0.5), 0.05),
        (0.3, 0.0),
    )
    updated = [
        adamw(
            shards[member],
            stacked[member],
            firsts[member],
            seconds[member],
            settings[member][0],
            settings[member][1],
        )
        for member in range(5)
    ]
    d_tokens = grad.reshape(images, SPAN, D)[:, :SEQ]
    return (
        output,
        d_tokens,
        updated[0][0],
        updated[1][0],
        updated[2][0],
        updated[3][0],
        updated[4][0],
        updated[0][1],
        updated[1][1],
        updated[2][1],
        updated[3][1],
        updated[4][1],
        updated[0][2],
        updated[1][2],
        updated[2][2],
        updated[3][2],
        updated[4][2],
    )


def solution(mesh):
    in_specs = (
        P(("node", "chip"), None, None),
        P(("node", "chip"), None, None),
        P(None, ("node", "chip"), None),
        P(None, ("node", "chip"), None),
        P(None, ("node", "chip"), None),
        P(None, ("node", "chip"), None),
        P(None, ("node", "chip")),
        P(None, ("node", "chip"), None),
        P(None, ("node", "chip"), None),
        P(None, ("node", "chip"), None),
        P(None, ("node", "chip"), None),
        P(None, ("node", "chip")),
        P(None, ("node", "chip"), None),
        P(None, ("node", "chip"), None),
        P(None, ("node", "chip"), None),
        P(None, ("node", "chip"), None),
        P(None, ("node", "chip")),
    )
    out_specs = (
        P(("node", "chip"), None, None),
        P(("node", "chip"), None, None),
        P(None, ("node", "chip"), None),
        P(None, ("node", "chip"), None),
        P(None, ("node", "chip"), None),
        P(None, ("node", "chip"), None),
        P(None, ("node", "chip")),
        P(None, ("node", "chip"), None),
        P(None, ("node", "chip"), None),
        P(None, ("node", "chip"), None),
        P(None, ("node", "chip"), None),
        P(None, ("node", "chip")),
        P(None, ("node", "chip"), None),
        P(None, ("node", "chip"), None),
        P(None, ("node", "chip"), None),
        P(None, ("node", "chip"), None),
        P(None, ("node", "chip")),
    )
    return jax.shard_map(
        functools.partial(on_device, Shape(mesh)), mesh=mesh, in_specs=in_specs, out_specs=out_specs, check_vma=False
    )
```

time: 746 us -> 642 us (0.86)
  Pallas kernels: 685 us -> 594 us
  local copies, waits for them, and re-layouts: 34.5 us -> 25.3 us
    pallas_call x10 -> x4, Pallas kernels: 685 us -> 339 us  [beside(): pl.pallas_call(body, grid=(grid,), in_specs=in_specs, out_specs=out_specs...]
    pallas_call x0 -> x1, Pallas kernels: none -> 254 us  [forward(): pl.pallas_call(functools.partial(forward_kernel, shape, layers), grid=(to...]
where the time goes in v3:
time: 642 us; the launch traced here: 638 us
  Pallas kernels  594 us (93%)
  local copies, waits for them, and re-layouts  25.3 us (4%)
  other arithmetic  16.9 us (3%)
    pallas_call x4, Pallas kernels, beside(): pl.pallas_call(body, grid=(grid,), in_specs=in_specs, out_specs=out_specs...  339 us
    pallas_call x1, Pallas kernels, forward(): pl.pallas_call(functools.partial(forward_kernel, shape, layers), grid=(to...  254 us

profile of v3, /device:TPU:0, one launch (start us, length us, event | category | flops | bytes accessed | tf_op | source)
XLA Modules:
  0.0 637.7 jit_solution(16672723939797059043)
XLA Ops:
  0.7 2.0 pad_convert_fusion.1
  2.7 3.0 copy.40
  7.1 0.9 convert_element_type.43.refs_2_
  8.0 1.0 convert.23
  11.7 0.9 convert_element_type.49.refs_6_
  12.6 254.2 %forward.1 = (bf16[2,640,1024]{2,1,0:T(8,128)(2,1)}, bf16[2,640,1024]{2,1,0:T(8,128)(2,1)}, bf16[2,640,1024]{2,1,0:T(8,128)(2,1)}, bf16[2,640,1024]{2,1,0:T(8,12...) custom-call(f32[640,1024]{1,0:T(8,128)} %bitcast.214, ...), custom_call_target="tpu_custom_call" | custom-call | tf_op jit(solution)/shard_map/forward/pallas_call | solution.py:627
  266.9 1.5 slice.397
  268.3 1.9 copy.46
  271.0 3.0 copy.44
  274.7 54.5 %mlp_backward.2 = (bf16[4096,1024]{1,0:T(8,128)(2,1)}, f32[640,1024]{1,0:T(8,128)}, bf16[640,1024]{1,0:T(8,128)(2,1)}, f32[16,1024]{1,0:T(8,128)}, f32[1,4096]{1...) custom-call(f32[640,1024]{1,0:T(8,128)} %bitcast.216, ...), custom_call_target="tpu_custom_call" | custom-call | tf_op jit(solution)/shard_map/mlp_backward/pallas_call | solution.py:358
  329.7 1.4 reduce.6
  331.1 0.9 pad_maximum_fusion.5
  332.6 84.7 %attention_backward.2 = (f32[640,1024]{1,0:T(8,128)}, f32[16,1024]{1,0:T(8,128)}, f32[14,32,256]{2,1,0:T(8,128)}, f32[3,128,128]{2,1,0:T(8,128)}, bf16[4,128,128...) custom-call(f32[640,1024]{1,0:T(8,128)} %get-tuple-element.105.refs_, ...), custom_call_target="tpu_custom_call" | custom-call | tf_op jit(solution)/shard_map/attention_backward/pallas_call | solution.py:358
  417.4 65.2 %mlp_backward.3 = (bf16[4096,1024]{1,0:T(8,128)(2,1)}, f32[640,1024]{1,0:T(8,128)}, bf16[640,1024]{1,0:T(8,128)(2,1)}, f32[16,1024]{1,0:T(8,128)}, f32[1,4096]{1...) custom-call(f32[640,1024]{1,0:T(8,128)} %get-tuple-element.128.refs_, ...), custom_call_target="tpu_custom_call" | custom-call | tf_op jit(solution)/shard_map/mlp_backward/pallas_call | solution.py:358
  482.6 1.4 reduce.7
  484.1 1.5 pad_maximum_fusion.4.refs_6_
  485.6 135.1 %attention_backward.3 = (f32[640,1024]{1,0:T(8,128)}, f32[16,1024]{1,0:T(8,128)}, f32[32,32,256]{2,1,0:T(8,128)}, f32[8,128,128]{2,1,0:T(8,128)}, f32[32,1024]{1,0:T(8,128)}) custom-call(f32[640,1024]{1,0:T(8,128)} %get-tuple-element.142.refs_0_, bf16[640,1024]{1,0:T(8,128)(2,1)} %get-tuple-element.143.refs_1_, f32[640,1024]{1,0:T(8,128)} %bitcast.215, ...), custom_call_target="tpu_custom_call" | custom-call | tf_op jit(solution)/shard_map/attention_backward/pallas_call | solution.py:358
  620.7 2.0 slice.398
  622.7 2.9 copy.47
  627.0 1.8 multiply_subtract_fusion.2
  628.9 1.0 multiply_subtract_fusion.3
  630.7 2.2 multiply_subtract_fusion.1
  633.1 1.0 copy-done.2
  634.4 2.2 multiply_subtract_fusion
  (145 shorter events, 9.8 us)
Async XLA Ops:
  2.6 3.0 copy-start.25
  2.6 4.2 copy-start.3
  5.7 4.0 copy-start
  6.9 3.7 copy-start.1
  266.8 3.4 copy-start.4
  271.0 3.0 copy-start.23
  417.4 65.2 %copy-start.19 = (f32[16,1024]{1,0:T(8,128)S(1)}, f32[16,1024]{1,0:T(8,128)}, u32[]{:S(2)}) copy-start(f32[16,1024]{1,0:T(8,128)} %get-tuple-element.110) | copy-start | bytes 196612
  417.4 65.2 %copy-start.24 = (f32[16,1024]{1,0:T(8,128)S(1)}, f32[16,1024]{1,0:T(8,128)}, u32[]{:S(2)}) copy-start(f32[16,1024]{1,0:T(8,128)} %get-tuple-element.146) | copy-start | bytes 196612
  622.7 3.0 copy-start.20
  622.7 3.1 copy-start.14
  622.7 3.2 copy-start.15
  622.7 3.3 copy-start.9
  627.0 1.9 copy-start.10
  627.0 1.9 copy-start.17
  627.0 1.9 copy-start.18
  628.8 1.8 copy-start.6
  630.7 2.2 copy-start.21
  630.7 2.2 copy-start.16
  630.7 2.3 copy-start.13
  630.7 2.4 copy-start.8
  634.4 2.2 copy-start.22
  634.4 2.4 copy-start.26
  634.4 2.4 copy-start.27
  634.4 2.4 copy-start.28
  (5 other events, 6.9 us)

commit v4 on v3

--- a/solution.py
+++ b/solution.py
@@ -204,7 +204,7 @@
 ANYWHERE = pl.BlockSpec(memory_space=pl.ANY)
 
 
-ORDERS = (("x", "q", "p"), ("q", "x", "p")) * 2 + (("x", "p", "q"), ("q", "p", "x"))
+ORDERS = (("x", "q", "p"), ("q", "x", "p"))
 
 
 class Piece:
@@ -398,6 +398,12 @@
     return [slice(i, i + step) for i in range(0, rows, step)]
 
 
+def fill_rows(rows, tokens):
+    rows[...] = jnp.zeros_like(rows)
+    for i in range(tokens.shape[0]):
+        rows[i * SPAN : i * SPAN + SEQ, :] = tokens[i].astype(FULL)
+
+
 def row(vec, index):
     return vec[index : index + 1, :]
 
@@ -471,7 +477,7 @@
     count = 4 * layers
     tokens, packed, *sources = refs[: 2 + count]
     refs = refs[2 + count :]
-    a_out, q_out, k_out, v_out, mixed_out, branch_out, mid_out, c_out, u_out, act_out, down_out, vec_out, next_out, low_out = refs[:14]
+    a_out, q_out, k_out, v_out, mixed_out, branch_out, mid_out, c_out, u_out, act_out, down_out, hidden_out, vec_out, low_out = refs[:14]
     gathered, refs = refs[14 : 14 + count], refs[14 + count :]
     h, act, vec = refs[:3]
     slots, sums, (send, recv, loaded) = refs[3:7], refs[7:14], refs[14:]
@@ -521,11 +527,12 @@
 
     @pl.when(at == 0)
     def _():
-        h[...] = tokens[...]
+        fill_rows(h, tokens)
 
     @pl.when(live & (item == 0))
     def _():
         vec[...] = vec_out[pl.ds(base, ROWS), :]
+        hidden_out[0] = h[...]
         for t in tiles(rows):
             normal, _ = normalise(h[t, :])
             a_out[0, t, :] = (normal * line(GAIN_A) + line(SHIFT_A)).astype(LOW)
@@ -582,17 +589,14 @@
         down_out[0, :, group] = down
         h[:, group] = mid_out[0, :, group] + vec[SCALE_M : SCALE_M + 1, group] * down
 
-    @pl.when(at == ITEMS - 1)
-    def _():
-        next_out[...] = h[...]
-
     @pl.when(at == total - 1)
     def _():
-        low_out[...] = h[...].astype(LOW)
+        for i in range(low_out.shape[0]):
+            low_out[i] = h[i * SPAN : i * SPAN + SEQ, :].astype(LOW)
 
 
 def forward(shape, layers, tokens, packed, sources, number):
-    rows = tokens.shape[0]
+    rows = tokens.shape[0] * SPAN
     total = layers * ITEMS
 
     def spot(s):
@@ -613,8 +617,8 @@
     tile = lambda item: jnp.clip(item - N_IN - 1, 0, N_UP - 1)
     qkv = [out(D, LOW, group, GROUP)] * 3
     outs = [out(D, LOW)] + qkv + [out(D, LOW), out(D, FULL), out(D, FULL), out(D, LOW)]
-    outs += [out(FF, FULL, tile, FF_TILE), out(FF, LOW, tile, FF_TILE), out(D, FULL)]
-    outs += [one(packed.shape, FULL), one((rows, D), FULL), one((rows, D), LOW)]
+    outs += [out(FF, FULL, tile, FF_TILE), out(FF, LOW, tile, FF_TILE), out(D, FULL), out(D, FULL)]
+    outs += [one(packed.shape, FULL), one(tokens.shape, LOW)]
     outs += [(jax.ShapeDtypeStruct(shape.grid + b.shape, LOW), ANYWHERE) for b in sources]
     sizes = shape.sizes
     tasks = 2 * total + 1
@@ -627,7 +631,7 @@
     return pl.pallas_call(
         functools.partial(forward_kernel, shape, layers),
         grid=(total + AHEAD,),
-        in_specs=[whole((rows, D)), whole(packed.shape)] + [ANYWHERE] * len(sources),
+        in_specs=[whole(tokens.shape), whole(packed.shape)] + [ANYWHERE] * len(sources),
         out_specs=[o[1] for o in outs],
         out_shape=[o[0] for o in outs],
         scratch_shapes=[pltpu.VMEM((rows, D), FULL), pltpu.VMEM((rows, FF), LOW), pltpu.VMEM((ROWS, D), FULL)]
@@ -657,14 +661,17 @@
     return jnp.sum(values, axis=0, keepdims=True)
 
 
-def mlp_bwd(tick, g, down, mid, branch, c, vec, u, act, wu, wd, g_down, d_mid, db_out, sums, d_bias_u, dd, stage):
+def mlp_bwd(tick, given, down, mid, branch, c, vec, u, act, wu, wd, g_down, d_mid, db_out, sums, d_bias_u, dd, stage, *own):
     step, last = pl.program_id(0), pl.num_programs(0) - 1
-    rows = g.shape[0]
+    rows = mid.shape[0]
+    g = own[0] if own else given
     tick(0)
 
     @pl.when(step == 0)
     def _():
         sums[...] = jnp.zeros_like(sums)
+        if own:
+            fill_rows(g, given)
         for t in tiles(rows):
             grad = g[t, :]
             scaled = grad * row(vec, SCALE_M)
@@ -700,7 +707,7 @@
 
 
 def mlp_backward(layer, g, down, mid, branch, c, vec, u, act, w_up, w_down, shape, transfer, number):
-    rows = g.shape[0]
+    rows = mid.shape[1]
     f32, low = lambda s: jax.ShapeDtypeStruct(s, FULL), lambda s: jax.ShapeDtypeStruct(s, LOW)
     full = whole((rows, D))
     tile = columns_of(layer, rows, FF_TILE)
@@ -712,14 +719,15 @@
         number=number,
         grid=steps,
         inputs=[g, down, mid, branch, c, vec, u, act, w_up, w_down],
-        in_specs=[full] + [whole_of(layer, rows)] * 4
+        in_specs=[whole(g.shape)] + [whole_of(layer, rows)] * 4
         + [whole(vec.shape), tile, tile, columns(D, FF_TILE), lines(FF_TILE, D)],
         out_specs=[lines(FF_TILE, D), full, full, whole((ROWS, D)), columns(1, FF_TILE)],
         out_shape=[low((FF, D)), f32((rows, D)), low((rows, D)), f32((ROWS, D)), f32((1, FF))],
         scratch=[
             pltpu.VMEM((rows, D), LOW),
             pltpu.VMEM((steps,) + shape.grid + (D // shape.devices, FF_TILE), LOW),
-        ],
+        ]
+        + [pltpu.VMEM((rows, D), FULL)] * (g.ndim == 3),
         name="mlp_backward",
     )
 
@@ -784,7 +792,7 @@
 
 
 def attention_backward(layer, d_mid, db, h, a, vec, mixed, rest, q, k, v, w_in, w_out, shape, transfer, number):
-    rows = h.shape[0]
+    rows = d_mid.shape[0]
     n = D // GROUP
     f32 = lambda s: jax.ShapeDtypeStruct(s, FULL)
     full = whole((rows, D))
@@ -796,8 +804,9 @@
         number=number,
         grid=n,
         inputs=[d_mid, db, h, a, vec, mixed, rest, q, k, v, w_in, w_in, w_in, w_out],
-        in_specs=[full] * 3
-        + [whole_of(layer, rows), whole(vec.shape), whole_of(layer, rows), whole(rest.shape)]
+        in_specs=[full] * 2
+        + [whole_of(layer, rows)] * 2
+        + [whole(vec.shape), whole_of(layer, rows), whole(rest.shape)]
         + [cols] * 3
         + [pl.BlockSpec((D, GROUP), lambda j, m=m: (0, 3 * j + m)) for m in range(3)]
         + [lines(GROUP, D)],
@@ -834,10 +843,6 @@
 
 def shape_blocks(shape, term):
     return term.reshape(shape.grid + (term.shape[0] // shape.devices, term.shape[1]))
-
-
-def spread_rows(tokens):
-    return jnp.pad(tokens, ((0, 0), (0, SPAN - SEQ), (0, 0))).reshape(-1, D)
 
 
 def adamw(weight, gradient, first, second, rate, decay):
@@ -880,18 +885,15 @@
     for layer in range(layers):
         by_group = shards[0][layer].reshape(-1, 3, D // GROUP, GROUP).transpose(0, 2, 1, 3).reshape(-1, 3 * D)
         sources += [m.astype(LOW) for m in (by_group, w_attn_out[layer], w_mlp_in[layer], w_mlp_out[layer])]
-    first = spread_rows(tokens.astype(FULL))
-    outs = forward(shape, layers, first, packed, sources, 1)
-    vec_rows, second, low = outs[11:14]
+    outs = forward(shape, layers, tokens, packed, sources, 1)
+    hidden, vec_rows, low = outs[11:14]
     weights = [w.reshape(-1, w.shape[-1]) for w in outs[14:]]
     kept = []
     for layer in range(layers):
         a, q, k, v, mixed, branch, mid, c, u, act, down = outs[:11]
         vec = vec_rows[layer * ROWS : layer * ROWS + ROWS]
-        hidden = second if layer else first
         kept.append((vec, *weights[4 * layer : 4 * layer + 4], hidden, a, q, k, v, mixed, branch, mid, c, u, act, down))
-    output = low.reshape(images, SPAN, D)[:, :SEQ]
-    grad = spread_rows(cotangent.astype(FULL))
+    grad = cotangent
     high, deep = D // shape.devices, FF // shape.devices
     pieces, rest, left, number, order = [], jnp.zeros((0, D), FULL), [], 10, 0
     everything = [[[None] * (2 * N_UP), [None] * N_DOWN * 2, [None] * 4 * N_IN] for _ in range(layers)]
@@ -986,7 +988,7 @@
     ]
     d_tokens = grad.reshape(images, SPAN, D)[:, :SEQ]
     return (
-        output,
+        low,
         d_tokens,
         updated[0][0],
         updated[1][0],

time: 642 us -> 633 us (0.986)
  no operation moved by 1% of the time
where the time goes in v4:
time: 633 us; the launch traced here: 630 us
  Pallas kernels  590 us (93%)
  local copies, waits for them, and re-layouts  23.3 us (4%)
  other arithmetic  15 us (2%)
    pallas_call x4, Pallas kernels, beside(): pl.pallas_call(body, grid=(grid,), in_specs=in_specs, out_specs=out_specs...  336 us
    pallas_call x1, Pallas kernels, forward(): pl.pallas_call(functools.partial(forward_kernel, shape, layers), grid=(to...  254 us
    unnamed x114, local copies, waits for them, and re-layouts  13.7 us

profile of v4, /device:TPU:0, one launch (start us, length us, event | category | flops | bytes accessed | tf_op | source)
XLA Modules:
  0.0 629.8 jit_solution(6668220468198899735)
XLA Ops:
  0.7 2.7 copy.42.refs_0_
  5.7 0.9 convert_element_type.38.refs_2_
  6.6 1.0 convert.17
  8.2 0.8 slice_bitcast_fusion.1
  9.1 0.8 slice_bitcast_fusion
  10.2 0.9 convert_element_type.44.refs_6_
  11.1 254.0 %forward.1 = (bf16[2,640,1024]{2,1,0:T(8,128)(2,1)}, bf16[2,640,1024]{2,1,0:T(8,128)(2,1)}, bf16[2,640,1024]{2,1,0:T(8,128)(2,1)}, bf16[2,640,1024]{2,1,0:T(8,12...) custom-call(bf16[4,145,1024]{2,1,0:T(8,128)(2,1)} %copy.42.refs_0_, ...), custom_call_target="tpu_custom_call" | custom-call | tf_op jit(solution)/shard_map/forward/pallas_call | solution.py:631
  265.1 3.3 copy.45
  268.4 1.4 copy.43.refs_0_
  270.4 51.8 %mlp_backward.2 = (bf16[4096,1024]{1,0:T(8,128)(2,1)}, f32[640,1024]{1,0:T(8,128)}, bf16[640,1024]{1,0:T(8,128)(2,1)}, f32[16,1024]{1,0:T(8,128)}, f32[1,4096]{1...) custom-call(bf16[4,145,1024]{2,1,0:T(8,128)(2,1)} %copy.43.refs_0_, ...), custom_call_target="tpu_custom_call" | custom-call | tf_op jit(solution)/shard_map/mlp_backward/pallas_call | solution.py:358
  322.8 1.4 reduce.6
  324.2 0.9 pad_maximum_fusion.5
  325.7 81.1 %attention_backward.2 = (f32[640,1024]{1,0:T(8,128)}, f32[16,1024]{1,0:T(8,128)}, f32[14,32,256]{2,1,0:T(8,128)}, f32[3,128,128]{2,1,0:T(8,128)}, bf16[4,128,128...) custom-call(f32[640,1024]{1,0:T(8,128)} %get-tuple-element.105.refs_, ...), custom_call_target="tpu_custom_call" | custom-call | tf_op jit(solution)/shard_map/attention_backward/pallas_call | solution.py:358
  406.9 68.8 %mlp_backward.3 = (bf16[4096,1024]{1,0:T(8,128)(2,1)}, f32[640,1024]{1,0:T(8,128)}, bf16[640,1024]{1,0:T(8,128)(2,1)}, f32[16,1024]{1,0:T(8,128)}, f32[1,4096]{1...) custom-call(f32[640,1024]{1,0:T(8,128)} %get-tuple-element.128.refs_, ...), custom_call_target="tpu_custom_call" | custom-call | tf_op jit(solution)/shard_map/mlp_backward/pallas_call | solution.py:358
  475.7 1.4 reduce.7
  477.1 1.5 pad_maximum_fusion.4.refs_6_
  478.7 134.1 %attention_backward.3 = (f32[640,1024]{1,0:T(8,128)}, f32[16,1024]{1,0:T(8,128)}, f32[32,32,256]{2,1,0:T(8,128)}, f32[8,128,128]{2,1,0:T(8,128)}, f32[32,1024]{1,0:T(8,128)}) custom-call(f32[640,1024]{1,0:T(8,128)} %get-tuple-element.142.refs_0_, bf16[640,1024]{1,0:T(8,128)(2,1)} %get-tuple-element.143.refs_1_, f32[2,640,1024]{2,1,0:T(8,128)} %get-tuple-element.107.refs_2_, ...), custom_call_target="tpu_custom_call" | custom-call | tf_op jit(solution)/shard_map/attention_backward/pallas_call | solution.py:358
  612.8 2.0 slice.393
  614.8 2.9 copy.46
  619.2 1.8 multiply_subtract_fusion.2
  621.0 1.0 multiply_subtract_fusion.3
  622.8 2.2 multiply_subtract_fusion.1
  625.2 1.0 copy-done.2
  626.5 2.2 multiply_subtract_fusion
  (140 shorter events, 8.2 us)
Async XLA Ops:
  0.7 4.7 copy-start.3
  3.4 4.8 copy-start
  5.4 3.7 copy-start.1
  11.1 257.3 %copy-start.4 = (bf16[4,145,1024]{2,0,1:T(4,128)(2,1)S(1)}, bf16[4,145,1024]{2,0,1:T(4,128)(2,1)}, u32[]{:S(2)}) copy-start(bf16[4,145,1024]{2,0,1:T(4,128)(2,1)} %param.18) | copy-start | bytes 3563524
  265.1 4.7 copy-start.23
  406.9 68.8 %copy-start.19 = (f32[16,1024]{1,0:T(8,128)S(1)}, f32[16,1024]{1,0:T(8,128)}, u32[]{:S(2)}) copy-start(f32[16,1024]{1,0:T(8,128)} %get-tuple-element.110) | copy-start | bytes 196612
  406.9 68.8 %copy-start.24 = (f32[16,1024]{1,0:T(8,128)S(1)}, f32[16,1024]{1,0:T(8,128)}, u32[]{:S(2)}) copy-start(f32[16,1024]{1,0:T(8,128)} %get-tuple-element.146) | copy-start | bytes 196612
  614.8 3.0 copy-start.20
  614.8 3.1 copy-start.14
  614.8 3.2 copy-start.15
  614.8 3.3 copy-start.9
  619.2 1.9 copy-start.10
  619.2 1.9 copy-start.17
  619.2 1.9 copy-start.18
  620.9 1.8 copy-start.6
  622.8 2.2 copy-start.21
  622.8 2.2 copy-start.16
  622.8 2.3 copy-start.13
  622.8 2.4 copy-start.8
  624.9 1.6 copy-start.7
  626.5 2.2 copy-start.22
  626.5 2.4 copy-start.25
  626.5 2.4 copy-start.26
  626.5 2.4 copy-start.27
  (4 other events, 5.3 us)
